TPU v7x, 128 devices: a whole 4x4x4 slice. The times are simulated.
128 devices in a mesh: camp: 16 (over y, z), tm: 8 (over x, core).
Axes of the slice: x: 4, y: 4, z: 4, core: 2. Of those that a mesh axis runs over, the one named last changes fastest.
Arguments:
- primal_start: float32 [32, 192, 32768], P('tm', None, 'camp'), may hold values from 0 to 2
- supply_start: float32 [32, 192], P('tm'), may hold values from 0 to 1
- reach_start: float32 [192, 32768], P(None, 'camp'), may hold values from 0 to 1
- spend_start: float32 [32, 32768], P('tm', 'camp'), may hold values from 0 to 0.05
- value: float32 [192, 32768], P(None, 'camp'), may hold values from 0.5 to 2
- share: float32 [192, 32768], P(None, 'camp'), may hold values from 0.05 to 1
- price: float32 [192, 32768], P(None, 'camp'), may hold values from 0.25 to 4
- reach_cap: float32 [192, 32768], P(None, 'camp'), may hold values from 0.5 to 4
- spend_limit: float32 [32768], P('camp'), may hold values from 768 to 3072
- supply: float32 [32, 192], P('tm'), may hold values from 4096 to 16384
- eligible: int32 [24, 32768], P(None, 'camp'), may hold values 0 or 1
- start_slot: int32 [32768], P('camp'), may hold values from 0 to 15
- active_span: int32 [32768], P('camp'), may hold values from 8 to 16
Outputs:
- primal: float32 [32, 192, 32768], P('tm', None, 'camp')
- supply_dual: float32 [32, 192], P('tm')
- reach_dual: float32 [192, 32768], P(None, 'camp')
- spend_dual: float32 [32, 32768], P('tm', 'camp')
All inputs are finite; a program needn't handle non-finite values. No bound on the sum of `eligible` on one device may be relied on, other than what follows from the above.
Results may differ from a plain program's by a relative error of at most 0.0001.
Values sent between devices are 32-bit elements; how exact they have to be, the bound alone decides.
A program may use at most 64 MiB of HBM per device.

v0:
```python
import jax
import jax.numpy as jnp
from jax import lax
from jax.sharding import PartitionSpec as P

S = 192
SEG_BLOCK = 8
SLOTS = 32
ITERS = 2


def carried_in(value, axis, join, neutral, backward):
    count, mine = (lax.axis_size(axis), lax.axis_index(axis))
    pieces = lax.all_gather(value, axis)
    if backward:
        pieces = pieces[::-1]
        mine = count - 1 - mine
    so_far = jnp.full_like(value, 0) + jnp.asarray(neutral, value.dtype)

    def lap(position, so_far):
        longer = join(so_far, pieces[position])
        return jnp.where(position < mine, longer, so_far)

    return lax.fori_loop(0, count - 1, lap, so_far)


def adding(first, second):
    return first + second


def later_total(totals):
    return carried_in(totals, "tm", adding, jnp.zeros_like(totals), True)


def earlier_total(totals):
    return carried_in(totals, "tm", adding, jnp.zeros_like(totals), False)


def shards(
    primal_start,
    supply_start,
    reach_start,
    spend_start,
    value,
    share,
    price,
    reach_cap,
    spend_limit,
    supply,
    eligible,
    start_slot,
    active_span,
):
    slot_dev = primal_start.shape[0]
    camp_dev = primal_start.shape[2]
    total_camp = lax.axis_size("camp") * camp_dev
    slots_here = (lax.axis_index("tm") * slot_dev + lax.iota(jnp.int32, slot_dev))[:, None]
    begin = start_slot[None, :]
    finish = begin + active_span[None, :]
    active = ((slots_here >= begin) & (slots_here < finish)).astype(jnp.float32)
    elig = jnp.repeat(eligible.astype(jnp.float32), SEG_BLOCK, axis=0)
    allow = active[:, None, :] * elig[None]
    frac = jnp.clip(
        (slots_here + 1 - begin).astype(jnp.float32) / active_span[None, :].astype(jnp.float32),
        0.0,
        1.0,
    )
    cap = spend_limit[None, :] * frac
    sig_supply = 4.0 / total_camp
    sig_reach = 1.0 / (2 * SLOTS)
    sig_spend = 1.0 / (S * SLOTS * SLOTS)
    anchor = (primal_start, supply_start, reach_start, spend_start)
    state = anchor
    for step in range(ITERS):
        keep = (step + 1.0) / (step + 2.0)

        def blend(fresh, older, start):
            return keep * (2.0 * fresh - older) + (1.0 - keep) * start

        primal, sdual, rdual, pdual = state
        rev_local = jnp.flip(jnp.cumsum(jnp.flip(pdual, 0), 0), 0)
        zrev = rev_local + later_total(jnp.sum(pdual, axis=0))[None]
        grad = (
            -value[None]
            + share[None] * sdual[:, :, None]
            + rdual[None]
            + price[None] * zrev[:, None, :]
        )
        nxt = jnp.maximum(primal - 0.5 * grad, 0.0) * allow
        bar = 2.0 * nxt - primal
        used = lax.psum(jnp.sum(share[None] * bar, axis=2), "camp")
        new_s = jnp.maximum(sdual + sig_supply * (used - supply), 0.0)
        local_deliv = jnp.sum(bar, axis=0)
        deliv = lax.psum(local_deliv, "tm")
        new_r = jnp.maximum(rdual + sig_reach * (deliv - reach_cap), 0.0)
        out_r = blend(new_r, rdual, reach_start)
        per_slot = jnp.sum(price[None] * bar, axis=1)
        spend = jnp.cumsum(per_slot, 0) + earlier_total(jnp.sum(per_slot, axis=0))[None]
        new_p = jnp.maximum(pdual + sig_spend * (spend - cap), 0.0)
        state = (
            blend(nxt, primal, primal_start),
            blend(new_s, sdual, supply_start),
            out_r,
            blend(new_p, pdual, spend_start),
        )
    return (state[0], state[1], state[2], state[3])


def solution(mesh):
    in_specs = (
        P("tm", None, "camp"),
        P("tm", None),
        P(None, "camp"),
        P("tm", "camp"),
        P(None, "camp"),
        P(None, "camp"),
        P(None, "camp"),
        P(None, "camp"),
        P("camp"),
        P("tm", None),
        P(None, "camp"),
        P("camp"),
        P("camp"),
    )
    out_specs = (P("tm", None, "camp"), P("tm", None), P(None, "camp"), P("tm", "camp"))
    return jax.shard_map(shards, mesh=mesh, in_specs=in_specs, out_specs=out_specs, check_vma=False)
```

profile of v0, /device:TPU:1, one launch (start us, length us, event | category | flops | bytes accessed | tf_op | source)
XLA Modules:
  0.0 209.9 jit_solution(11748764640777813317)
XLA Ops:
  7.2 0.0 all-reduce.3.cloned.1.call-start
  7.2 5.6 %rev.19 = f32[4,2048]{1,0:T(4,128)S(1)} reverse(f32[4,2048]{1,0:T(4,128)} %param.24), dimensions={0} | reverse | bytes 65536 | tf_op jit(solution)/shard_map/jit(_flip)/rev | solution.py:81
  12.9 0.8 reduce_sum.90
  13.7 14.4 %all-gather = f32[16384]{0:T(1024)S(1)} all-gather(f32[2048]{0:T(1024)S(1)} %reduce_sum.90), channel_id=2, replica_groups=mesh['camp'=16,'tm'=8] {'tm'}, dimensions={0}, use_global_device_ids=true | all-gather | bytes 73728 | tf_op jit(solution)/shard_map/all_gather | solution.py:14
  28.1 0.3 rev.21
  28.4 0.4 while.56
  28.8 0.1 reduce_window_sum.22
  28.8 0.4 rev.20
  29.3 0.9 convert_element_type.18
  30.2 0.0 copy-start.7
  30.2 0.0 copy-start.11
  30.2 0.0 copy-start.5
  30.2 0.2 broadcast_bitcast_fusion
  30.4 0.0 copy-start.1
  30.4 0.0 copy-start.4
  30.4 0.0 copy-start.8
  30.4 1.7 neg.5
  32.1 0.0 copy-done.7
  32.1 0.0 copy-done.11
  32.2 0.0 copy-start.2
  32.2 0.1 and_convert_fusion
  32.3 0.0 copy-done.5
  32.3 0.4 copy-done.1
  32.6 0.5 copy-done.4
  33.1 0.0 copy-done.8
  33.1 10.1 %multiply_reduce_fusion.4 = (f32[2048]{0:T(1024)S(1)}, f32[4,2048]{1,0:T(4,128)S(1)}, f32[4,192]{1,0:T(4,128)S(1)}, f32[192,2048]{1,0:T(8,128)}, f32[4,192,2048]{2,1,0:T(8,128)}) fusion(f32[192,2048]{1,0:T(8,128)S(1)} %copy-done.4, f32[192,2048]{1,0:T(8,128)S(1)} %copy-done.5, f32[4,192,2048]{2,1,0:T(8,128)} %param.21, ...), kind=kLoop, calls=%fused_computation.19 | loop fusion | flops 27907328 | bytes 22132736 | tf_op jit(solution)/shard_map/reduce_sum | solution.py:98
  43.3 0.0 copy-done.2
  43.3 0.0 copy-start.6
  43.3 0.0 copy-start.9
  43.3 0.0 copy-start.10
  43.3 0.0 all-reduce.3.cloned.1.call-update
  43.3 0.0 all-reduce.5.cloned.1.call-start
  43.4 12.7 %all-gather.1 = f32[16384]{0:T(1024)S(1)} all-gather(f32[2048]{0:T(1024)S(1)} %get-tuple-element.386), channel_id=3, replica_groups=mesh['camp'=16,'tm'=8] {'tm'}, dimensions={0}, use_global_device_ids=true | all-gather | bytes 73728 | tf_op jit(solution)/shard_map/all_gather | solution.py:14
  56.2 0.4 while.57
  56.5 0.1 reduce_window_sum.23
  56.6 0.0 copy-done.6
  56.6 0.0 copy-done.9
  56.6 0.1 multiply_reduce_fusion.6
  56.7 12.7 %all-gather.2 = f32[16384]{0:T(1024)S(1)} all-gather(f32[2048]{0:T(1024)S(1)} %get-tuple-element.425), channel_id=4, replica_groups=mesh['camp'=16,'tm'=8] {'tm'}, dimensions={0}, use_global_device_ids=true | all-gather | bytes 73728 | tf_op jit(solution)/shard_map/all_gather | solution.py:14
  69.5 0.3 rev.24
  69.8 0.4 while.58
  70.2 0.4 reverse.3
  70.6 0.1 reduce_window_sum.27
  70.7 0.4 rev.23
  71.1 34.7 %psum.28 = f32[4,192]{1,0:T(4,128)S(1)} all-reduce(f32[4,192]{1,0:T(4,128)S(1)} %get-tuple-element.390), channel_id=1, replica_groups=mesh['camp'=16,'tm'=8] {'camp'}, use_global_device_ids=true, to_apply=%region_5.6 | all-reduce | flops 768 | bytes 6144 | tf_op jit(solution)/shard_map/psum | solution.py:91
  105.9 0.0 copy-done.10
  105.9 0.9 all-reduce.3.cloned.1.call-done
  106.8 0.0 copy-start
  106.8 2.5 %fusion.4 = f32[192,2048]{1,0:T(8,128)S(1)} fusion(f32[192,2048]{1,0:T(8,128)S(1)} %copy-done.1, f32[192,2048]{1,0:T(8,128)} %all-reduce.3.cloned.1.call-done, f32[192,2048]{1,0:T(8,128)} %param.28), kind=kLoop, calls=%fused_computation.22 | loop fusion | flops 3145728 | bytes 6291456 | tf_op jit(solution)/shard_map/add | solution.py:78
  109.4 1.2 copy-done
  110.6 11.5 %multiply_reduce_fusion.2 = (f32[2048]{0:T(1024)S(1)}, f32[4,2048]{1,0:T(4,128)S(1)}, f32[192,2048]{1,0:T(8,128)}, f32[4,192]{1,0:T(4,128)S(1)}, f32[4,192,2048]{2,1,0:T(8,128)}) fusion(f32[192,2048]{1,0:T(8,128)} %param.27, f32[192,2048]{1,0:T(8,128)} %param.26, f32[192,2048]{1,0:T(8,128)S(1)} %broadcast_bitcast_fusion, f32[4,2048]{1,0:T(4,128)S(1)} %and_convert_fusion, ...), kind=kLoop, calls=%fused_computation.17 | loop fusion | flops 31053056 | bytes 28424192 | tf_op jit(solution)/shard_map/reduce_sum | solution.py:98
  122.0 19.1 %all-gather.3 = f32[16384]{0:T(1024)S(1)} all-gather(f32[2048]{0:T(1024)S(1)} %get-tuple-element.384), channel_id=5, replica_groups=mesh['camp'=16,'tm'=8] {'tm'}, dimensions={0}, use_global_device_ids=true | all-gather | bytes 73728 | tf_op jit(solution)/shard_map/all_gather | solution.py:14
  141.1 0.4 while.59
  141.5 0.1 reduce_window_sum.32
  141.6 0.0 all-reduce.5.cloned.1.call-update
  141.6 29.7 %psum.30 = f32[4,192]{1,0:T(4,128)S(1)} all-reduce(f32[4,192]{1,0:T(4,128)S(1)} %get-tuple-element.389), channel_id=1, replica_groups=mesh['camp'=16,'tm'=8] {'camp'}, use_global_device_ids=true, to_apply=%region_18.19 | all-reduce | flops 768 | bytes 6144 | tf_op jit(solution)/shard_map/psum | solution.py:91
  171.3 0.6 multiply_add_fusion.3
  171.9 0.7 multiply_add_fusion.2
  172.6 0.0 copy-start.3
  172.6 9.6 %multiply_add_fusion = f32[4,192,2048]{2,1,0:T(8,128)} fusion(f32[4,192,2048]{2,1,0:T(8,128)} %param.21, f32[4,192,2048]{2,1,0:T(8,128)} %get-tuple-element.424), kind=kLoop, calls=%fused_computation.15 | loop fusion | flops 4718592 | bytes 18874368 | tf_op jit(solution)/shard_map/add | solution.py:78
  182.2 16.9 %all-reduce.5.cloned.1.call-done = f32[192,2048]{1,0:T(8,128)} async-done(((f32[192,2048]{1,0:T(8,128)}), f32[192,2048]{1,0:T(8,128)}) %all-reduce.5.cloned.1.call-update) | async-done | bytes 1572880 | tf_op jit(solution)/shard_map/psum | solution.py:94
  199.1 0.0 copy-done.3
  199.1 3.9 %multiply_add_fusion.1 = f32[192,2048]{1,0:T(8,128)} fusion(f32[192,2048]{1,0:T(8,128)S(1)} %copy-done.1, f32[192,2048]{1,0:T(8,128)} %all-reduce.5.cloned.1.call-done, f32[192,2048]{1,0:T(8,128)S(1)} %copy-done.3, f32[192,2048]{1,0:T(8,128)} %all-reduce.3.cloned.1.call-done), kind=kLoop, calls=%fused_computation.23 | loop fusion | flops 6684672 | bytes 7864320 | tf_op jit(solution)/shard_map/add | solution.py:78
  (71 shorter events, 0.6 us)
Async XLA Ops:
  7.2 99.7 %all-reduce.3.cloned.1.call-start = ((), (), s32[]{:S(2)}) async-start(), calls=%async_computation | async-start | bytes 3145728 | tf_op jit(solution)/shard_map/psum | solution.py:94
  30.2 1.9 copy-start.7
  30.2 1.9 copy-start.11
  30.2 2.0 copy-start.5
  30.4 2.2 %copy-start.1 = (f32[192,2048]{1,0:T(8,128)S(1)}, f32[192,2048]{1,0:T(8,128)}, u32[]{:S(2)}) copy-start(f32[192,2048]{1,0:T(8,128)} %param.23) | copy-start | bytes 4718596
  30.4 2.7 %copy-start.4 = (f32[192,2048]{1,0:T(8,128)S(1)}, f32[192,2048]{1,0:T(8,128)}, u32[]{:S(2)}) copy-start(f32[192,2048]{1,0:T(8,128)} %param.27) | copy-start | bytes 4718596
  30.4 2.7 %copy-start.8 = (f32[4,192]{1,0:T(4,128)S(1)}, f32[4,192]{1,0:T(4,128)}, u32[]{:S(2)}) copy-start(f32[4,192]{1,0:T(4,128)} %param.22) | copy-start | bytes 9220
  32.2 11.1 %copy-start.2 = (f32[192,2048]{1,0:T(8,128)}, f32[192,2048]{1,0:T(8,128)S(1)}, u32[]{:S(2)}) copy-start(f32[192,2048]{1,0:T(8,128)S(1)} %neg.5) | copy-start | bytes 4718596
  43.3 13.3 %copy-start.6 = (f32[4,2048]{1,0:T(4,128)S(1)}, f32[4,2048]{1,0:T(4,128)}, u32[]{:S(2)}) copy-start(f32[4,2048]{1,0:T(4,128)} %param.24) | copy-start | bytes 98308
  43.3 13.3 %copy-start.9 = (f32[2048]{0:T(1024)S(1)}, f32[2048]{0:T(1024)}, u32[]{:S(2)}) copy-start(f32[2048]{0:T(1024)} %param.29) | copy-start | bytes 24580
  43.3 62.6 %copy-start.10 = (f32[4,192]{1,0:T(4,128)S(1)}, f32[4,192]{1,0:T(4,128)}, u32[]{:S(2)}) copy-start(f32[4,192]{1,0:T(4,128)} %param.30) | copy-start | bytes 9220
  43.3 155.8 %all-reduce.5.cloned.1.call-start = ((), (), s32[]{:S(2)}) async-start(), calls=%async_computation.1 | async-start | bytes 3145728 | tf_op jit(solution)/shard_map/psum | solution.py:94
  106.8 3.7 %copy-start = (f32[4,192,2048]{2,1,0:T(8,128)S(1)}, f32[4,192,2048]{2,1,0:T(8,128)}, u32[]{:S(2)}) copy-start(f32[4,192,2048]{2,1,0:T(8,128)} %get-tuple-element.427) | copy-start | bytes 18874372
  172.6 26.5 %copy-start.3 = (f32[192,2048]{1,0:T(8,128)S(1)}, f32[192,2048]{1,0:T(8,128)}, u32[]{:S(2)}) copy-start(f32[192,2048]{1,0:T(8,128)} %param.28) | copy-start | bytes 4718596
Sparse Core Ops, SparseCore 0:
  43.4 63.3 all-reduce.2
  141.7 57.3 all-reduce.4
where the time goes:
time: 212 us; the launch traced here: 210 us
  blocking collectives  123 us (58%)
  other arithmetic  43.1 us (20%)
  waiting for transfers between devices  17.9 us (8%)
  between operations  14.4 us (7%)
  local copies, waits for them, and re-layouts  10 us (5%)
    psum x2, blocking collectives, shards(): used = lax.psum(jnp.sum(share[None] * bar, axis=2), 'camp')  64.4 us
    all_gather x4, blocking collectives, carried_in(): pieces = lax.all_gather(value, axis)  59 us
    reduce_sum x2, other arithmetic, shards(): jnp.sum(per_slot, axis=0)  21.6 us
    psum x2, waiting for transfers between devices, shards(): deliv = lax.psum(local_deliv, 'tm')  17.8 us
    add x6, other arithmetic, blend(): return keep * (2.0 * fresh - older) + (1.0 - keep) * start  17.4 us
    rev x3, local copies, waits for them, and re-layouts, shards(): rev_local = jnp.flip(jnp.cumsum(jnp.flip(pdual, 0), 0), 0)  6.47 us
  transfers between devices with their start and end apart: 2, of which 2 were waited for; matrix products, arithmetic and copies ran while one was open for 6% of the time, Pallas kernels for 0%

commit v1 on v0

v1 whole, which is shorter than its diff:
```python
import jax
import jax.numpy as jnp
from jax import lax
from jax.experimental import pallas as pl
from jax.experimental.pallas import tpu as pltpu
from jax.sharding import PartitionSpec as P

S = 192
SEG_BLOCK = 8
SLOTS = 32
CAMPAIGNS = 32768
MESH = pl.DeviceIdType.MESH
HIGHEST = lax.Precision.HIGHEST

NT = 4
CD = 2048
NL = CD // 128
LT = 2
NC = NL // LT
QR = S // 4
NG = 2
GL = NL // NG
GC = NC // NG
BLOCKED = -1e30

SIG_SUPPLY = 4.0 / CAMPAIGNS
SIG_REACH = 1.0 / (2 * SLOTS)
SIG_SPEND = 1.0 / (S * SLOTS * SLOTS)


def kernel(
    x0_hbm, s0_ref, r0_hbm, p0_ref, value_hbm, share_hbm, price_hbm, rcap_hbm,
    limit_ref, supply_ref, elig_ref, begin_ref, span_ref,
    x_ref, s_out, r_ref, p_out,
    x0, value, share, price, r0, rcap,
    deliv, from_sib, from_x, r1,
    pen, sb, s8, s1, used, uz, uy,
    pk0, pk1, cap, live, zeff, spent, tstart, tots,
    ld, siba_s, siba_r, rs_s, rs_r, ag_s, ag_r, sibb_s, sibb_r,
    t0_s, t0_r, tot_s, tot_r, uz_s, uz_r, uy_s, uy_r,
):
    camp = lax.axis_index("camp")
    tm = lax.axis_index("tm")
    y, z = camp // 4, camp % 4
    x, core = tm // 2, tm % 2
    sib = (camp, x * 2 + 1 - core)
    xs = [(camp, ((x + d) % 4) * 2 + core) for d in (1, 2, 3)]
    tms = [(camp, (tm + d) % 8) for d in range(1, 8)]
    zs = [(y * 4 + (z + d) % 4, tm) for d in (1, 2, 3)]
    ys = [(((y + d) % 4) * 4 + z, tm) for d in (1, 2, 3)]
    mine = pl.multiple_of(x * QR, 8)

    def send(src, dst, ssem, rsem, to):
        return pltpu.make_async_remote_copy(
            src_ref=src, dst_ref=dst, send_sem=ssem, recv_sem=rsem, device_id=to, device_id_type=MESH
        )

    loads = []

    def load(src, dst):
        cp = pltpu.make_async_copy(src, dst, ld.at[len(loads)])
        cp.start()
        loads.append(cp)

    load(value_hbm, value)
    for t in range(NT):
        load(x0_hbm.at[t], x0.at[t])
    load(share_hbm, share)
    load(price_hbm, price)
    load(r0_hbm, r0)
    load(rcap_hbm.at[pl.ds(mine, QR)], rcap)

    barrier = pltpu.get_barrier_semaphore()
    greet = tms + zs + ys
    for to in greet:
        pl.semaphore_signal(barrier, inc=1, device_id=to, device_id_type=MESH)

    def spread_supply(rows):
        s8[0:NT, :] = rows * -0.5
        table = s8[...]
        for t in range(NT):
            pick = (lax.broadcasted_iota(jnp.int32, (8, 128), 0) == t).astype(jnp.float32)
            sb[t] = lax.dot_general(
                table, pick, (((0,), (0,)), ((), ())), precision=HIGHEST, preferred_element_type=jnp.float32
            )

    s8[...] = jnp.zeros_like(s8)
    spread_supply(s0_ref[...])
    for b in range(S // SEG_BLOCK):
        pen[b] = jnp.where(elig_ref[b : b + 1, :] > 0, 0.0, BLOCKED)
    for t in range(NT):
        for lt in range(NL):
            pk0[t, lt : lt + 1, :] = p0_ref[t : t + 1, lt * 128 : (lt + 1) * 128]
    begin = begin_ref[...]
    span = span_ref[...]
    for t in range(NT):
        slot = tm * NT + t
        live[t] = ((slot >= begin) & (slot < begin + span)).astype(jnp.float32)
        frac = jnp.clip((slot + 1 - begin).astype(jnp.float32) / span.astype(jnp.float32), 0.0, 1.0)
        cap[t] = limit_ref[...] * frac
    tstart[tm] = pk0[0] + pk0[1] + pk0[2] + pk0[3]
    loads[0].wait()

    def value_body(rb, carry):
        rows = pl.ds(pl.multiple_of(rb * 8, 8), 8)
        value[rows, :] = 0.5 * value[rows, :] + pen[rb]
        return carry

    lax.fori_loop(0, S // 8, value_body, 0)

    pl.semaphore_wait(barrier, len(greet))

    cps = [
        send(tstart.at[tm], tstart.at[tm], t0_s.at[d], t0_r.at[d], tms[d]) for d in range(7)
    ]
    for cp in cps:
        cp.start()

    def masked_total(parts, later):
        total = None
        for m in range(8):
            keep = (m > tm) if later else (m < tm)
            term = jnp.where(keep, parts(m), 0.0)
            total = term if total is None else total + term
        return total

    def set_zeff(duals, later, rows):
        run = later
        for t in reversed(range(NT)):
            run = run + duals[t]
            zeff[t, rows, :] = jnp.where(live[t, rows, :] > 0.0, -0.5 * run, BLOCKED)

    for cp in cps:
        cp.wait()
    set_zeff(
        [pk0[t] for t in range(NT)],
        masked_total(lambda m: tstart[m], True),
        slice(0, NL),
    )
    for cp in loads[1:]:
        cp.wait()
    used[...] = jnp.zeros_like(used)

    def comp(it, i):
        zb = [
            [jnp.broadcast_to(zeff[t, i * LT + l : i * LT + l + 1, :], (8, 128)) for l in range(LT)]
            for t in range(NT)
        ]

        def body(rb, acc):
            rows = pl.ds(pl.multiple_of(rb * 8, 8), 8)
            acc = list(acc)
            uses = [None] * NT
            for l in range(LT):
                cols = pl.ds((i * LT + l) * 128, 128)
                sh = share[rows, cols]
                pr = price[rows, cols]
                rd = r0[rows, cols] if it == 0 else r1[i, l, rows, :]
                base = value[rows, cols] - 0.5 * rd
                total = None
                for t in range(NT):
                    old = x0[t, rows, cols] if it == 0 else x_ref[t, rows, cols]
                    new = jnp.maximum((old + base) + (sh * sb[t, rows, :] + pr * zb[t][l]), 0.0)
                    bar = (new + new) - old
                    acc[t * LT + l] = acc[t * LT + l] + pr * bar
                    use = sh * bar
                    uses[t] = use if uses[t] is None else uses[t] + use
                    total = bar if total is None else total + bar
                    if it == 0:
                        x_ref[t, rows, cols] = new
                    else:
                        x_ref[t, rows, cols] = (2.0 / 3.0) * bar + (1.0 / 3.0) * x0[t, rows, cols]
                deliv[it, i, l, rows, :] = total
            for t in range(NT):
                used[t, rows, :] = used[t, rows, :] + uses[t]
            return tuple(acc)

        zero = jnp.zeros((8, 128), jnp.float32)
        acc = lax.fori_loop(0, S // 8, body, (zero,) * (NT * LT), unroll=2)
        for t in range(NT):
            for l in range(LT):
                spent[it, t, i * LT + l : i * LT + l + 1, :] = jnp.sum(acc[t * LT + l], axis=0, keepdims=True)

    pend = {}

    def siba_start(it, i):
        cp = send(deliv.at[it, i, 1 - core], from_sib.at[it, i], siba_s.at[it, i], siba_r.at[it, i], sib)
        cp.start()
        pend["a", it, i] = cp

    def rs_start(it, i):
        pend["a", it, i].wait()
        deliv[it, i, core] = deliv[it, i, core] + from_sib[it, i]
        cps = []
        for d in (1, 2, 3):
            theirs = pl.multiple_of(((x + d) % 4) * QR, 8)
            cps.append(
                send(
                    deliv.at[it, i, core, pl.ds(theirs, QR)],
                    from_x.at[it, i, d - 1],
                    rs_s.at[it, i, d - 1],
                    rs_r.at[it, i, d - 1],
                    xs[d - 1],
                )
            )
        for cp in cps:
            cp.start()
        pend["rs", it, i] = cps

    def out_cols(i, half):
        return pl.ds(pl.multiple_of((i * LT + half) * 128, 128), 128)

    def ag_start(it, i):
        for cp in pend["rs", it, i]:
            cp.wait()
        rows = pl.ds(mine, QR)
        cols = out_cols(i, core)
        total = deliv[it, i, core, rows, :] + from_x[it, i, 0] + from_x[it, i, 1] + from_x[it, i, 2]
        start = r0[rows, cols]
        if it == 0:
            r1[i, core, rows, :] = jnp.maximum(start + SIG_REACH * (total - rcap[:, cols]), 0.0)
            piece = r1.at[i, core, rows]
        else:
            old = r1[i, core, rows, :]
            new = jnp.maximum(old + SIG_REACH * (total - rcap[:, cols]), 0.0)
            r_ref[rows, cols] = (2.0 / 3.0) * (2.0 * new - old) + (1.0 / 3.0) * start
            piece = r_ref.at[rows, cols]
        cps = [
            send(piece, piece, ag_s.at[it, i, d], ag_r.at[it, i, d], xs[d]) for d in range(3)
        ]
        for cp in cps:
            cp.start()
        pend["ag", it, i] = cps

    def sibb_start(it, i):
        for cp in pend["ag", it, i]:
            cp.wait()
        piece = r1.at[i, core] if it == 0 else r_ref.at[:, out_cols(i, core)]
        cp = send(piece, piece, sibb_s.at[it, i], sibb_r.at[it, i], sib)
        cp.start()
        pend["b", it, i] = cp

    def sibb_wait(it, i):
        pend["b", it, i].wait()

    def used_z(it):
        total = None
        for t in range(NT):
            term = lax.dot_general(
                jnp.ones((8, 128), jnp.float32), used[t], (((1,), (1,)), ((), ())),
                precision=HIGHEST, preferred_element_type=jnp.float32,
            )
            row = lax.broadcasted_iota(jnp.int32, (8, S), 0) == t
            term = jnp.where(row, term, 0.0)
            total = term if total is None else total + term
        uz[it, z] = total
        cps = [send(uz.at[it, z], uz.at[it, z], uz_s.at[it, d], uz_r.at[it, d], zs[d]) for d in range(3)]
        for cp in cps:
            cp.start()
        pend["uz", it] = cps

    def used_y(it):
        for cp in pend["uz", it]:
            cp.wait()
        uy[it, y] = uz[it, 0] + uz[it, 1] + uz[it, 2] + uz[it, 3]
        cps = [send(uy.at[it, y], uy.at[it, y], uy_s.at[it, d], uy_r.at[it, d], ys[d]) for d in range(3)]
        for cp in cps:
            cp.start()
        pend["uy", it] = cps

    def used_end(it):
        for cp in pend["uy", it]:
            cp.wait()
        total = uy[it, 0] + uy[it, 1] + uy[it, 2] + uy[it, 3]
        total = total[0:NT, :]
        if it == 0:
            new = jnp.maximum(s0_ref[...] + SIG_SUPPLY * (total - supply_ref[...]), 0.0)
            s1[...] = new
            spread_supply(new)
        else:
            old = s1[...]
            new = jnp.maximum(old + SIG_SUPPLY * (total - supply_ref[...]), 0.0)
            s_out[...] = (2.0 / 3.0) * (2.0 * new - old) + (1.0 / 3.0) * s0_ref[...]

    def share_total(e, g, value):
        tots[e, g, tm] = value
        cps = [
            send(tots.at[e, g, tm], tots.at[e, g, tm], tot_s.at[e, g, d], tot_r.at[e, g, d], tms[d])
            for d in range(7)
        ]
        for cp in cps:
            cp.start()
        pend["t", e, g] = cps

    def wait_total(e, g, later):
        for cp in pend["t", e, g]:
            cp.wait()
        return masked_total(lambda m: tots[e, g, m], later)

    def spend_1(it, g):
        rows = slice(g * GL, (g + 1) * GL)
        share_total(2 * it, g, spent[it, 0, rows] + spent[it, 1, rows] + spent[it, 2, rows] + spent[it, 3, rows])

    def spend_2(it, g):
        rows = slice(g * GL, (g + 1) * GL)
        run = wait_total(2 * it, g, False)
        fresh = []
        for t in range(NT):
            run = run + spent[it, t, rows]
            old = pk0[t, rows] if it == 0 else pk1[t, rows]
            new = jnp.maximum(old + SIG_SPEND * (run - cap[t, rows]), 0.0)
            if it == 0:
                pk1[t, rows] = new
                fresh.append(new)
            else:
                res = (2.0 / 3.0) * (2.0 * new - old) + (1.0 / 3.0) * pk0[t, rows]
                for lt in range(GL):
                    c = (g * GL + lt) * 128
                    p_out[t : t + 1, c : c + 128] = res[lt : lt + 1, :]
        if it == 0:
            share_total(1, g, fresh[0] + fresh[1] + fresh[2] + fresh[3])

    def spend_3(g):
        rows = slice(g * GL, (g + 1) * GL)
        later = wait_total(1, g, True)
        set_zeff([pk1[t, rows] for t in range(NT)], later, rows)

    for i in range(NC):
        comp(0, i)
        siba_start(0, i)
        if i >= 1:
            rs_start(0, i - 1)
        if i == GC - 1:
            spend_1(0, 0)
    used_z(0)
    spend_1(0, 1)
    rs_start(0, NC - 1)
    for i in range(0, 2):
        ag_start(0, i)
    spend_2(0, 0)
    for i in range(2, 4):
        ag_start(0, i)
    used_y(0)
    spend_2(0, 1)
    for i in range(4, 6):
        ag_start(0, i)
    sibb_start(0, 0)
    spend_3(0)
    ag_start(0, 6)
    sibb_start(0, 1)
    used_end(0)
    used[...] = jnp.zeros_like(used)
    ag_start(0, 7)
    for i in range(NC):
        sibb_wait(0, i)
        if i + 2 < NC:
            sibb_start(0, i + 2)
        if i == GC:
            spend_3(1)
        comp(1, i)
        siba_start(1, i)
        if i >= 1:
            rs_start(1, i - 1)
        if i >= 4:
            ag_start(1, i - 4)
        if i == GC - 1:
            spend_1(1, 0)
    used_z(1)
    spend_1(1, 1)
    rs_start(1, NC - 1)
    sibb_start(1, 0)
    ag_start(1, 4)
    sibb_start(1, 1)
    ag_start(1, 5)
    sibb_start(1, 2)
    used_y(1)
    spend_2(1, 0)
    ag_start(1, 6)
    sibb_start(1, 3)
    spend_2(1, 1)
    ag_start(1, 7)
    sibb_start(1, 4)
    used_end(1)
    for i in range(5, NC):
        sibb_start(1, i)
    for i in range(NC):
        sibb_wait(1, i)


def shards(
    primal_start, supply_start, reach_start, spend_start, value, share, price, reach_cap,
    spend_limit, supply, eligible, start_slot, active_span,
):
    f32 = jnp.float32
    vmem = pl.BlockSpec(memory_space=pltpu.VMEM)
    anywhere = pl.BlockSpec(memory_space=pltpu.HBM)
    dma = pltpu.SemaphoreType.DMA
    outs = (
        pltpu.VMEM((NT, S, CD), f32),
        jax.ShapeDtypeStruct((NT, S), f32),
        pltpu.VMEM((S, CD), f32),
        jax.ShapeDtypeStruct((NT, CD), f32),
    )
    scratch = [
        pltpu.VMEM((NT, S, CD), f32),
        pltpu.VMEM((S, CD), f32),
        pltpu.VMEM((S, CD), f32),
        pltpu.VMEM((S, CD), f32),
        pltpu.VMEM((S, CD), f32),
        pltpu.VMEM((QR, CD), f32),
        pltpu.VMEM((2, NC, LT, S, 128), f32),
        pltpu.VMEM((2, NC, S, 128), f32),
        pltpu.VMEM((2, NC, 3, QR, 128), f32),
        pltpu.VMEM((NC, LT, S, 128), f32),
        pltpu.VMEM((S // SEG_BLOCK, 1, CD), f32),
        pltpu.VMEM((NT, S, 128), f32),
        pltpu.VMEM((8, S), f32),
        pltpu.VMEM((NT, S), f32),
        pltpu.VMEM((NT, S, 128), f32),
        pltpu.VMEM((2, 4, 8, S), f32),
        pltpu.VMEM((2, 4, 8, S), f32),
        pltpu.VMEM((NT, NL, 128), f32),
        pltpu.VMEM((NT, NL, 128), f32),
        pltpu.VMEM((NT, NL, 128), f32),
        pltpu.VMEM((NT, NL, 128), f32),
        pltpu.VMEM((NT, NL, 128), f32),
        pltpu.VMEM((2, NT, NL, 128), f32),
        pltpu.VMEM((8, NL, 128), f32),
        pltpu.VMEM((3, NG, 8, GL, 128), f32),
        dma((NT + 5,)),
        dma((2, NC)), dma((2, NC)),
        dma((2, NC, 3)), dma((2, NC, 3)),
        dma((2, NC, 3)), dma((2, NC, 3)),
        dma((2, NC)), dma((2, NC)),
        dma((7,)), dma((7,)),
        dma((3, NG, 7)), dma((3, NG, 7)),
        dma((2, 3)), dma((2, 3)),
        dma((2, 3)), dma((2, 3)),
    ]
    res = pl.pallas_call(
        kernel,
        out_shape=outs,
        in_specs=[anywhere, vmem, anywhere, vmem] + [anywhere] * 4 + [vmem] * 5,
        out_specs=(vmem, vmem, vmem, vmem),
        scratch_shapes=scratch,
        compiler_params=pltpu.CompilerParams(
            collective_id=0, has_side_effects=True, vmem_limit_bytes=44 * 2**20
        ),
    )(
        primal_start, supply_start, reach_start, spend_start, value, share, price, reach_cap,
        spend_limit.reshape(NL, 128), supply, eligible,
        start_slot.reshape(NL, 128), active_span.reshape(NL, 128),
    )
    return tuple(res)


def solution(mesh):
    in_specs = (
        P("tm", None, "camp"), P("tm", None), P(None, "camp"), P("tm", "camp"),
        P(None, "camp"), P(None, "camp"), P(None, "camp"), P(None, "camp"),
        P("camp"), P("tm", None), P(None, "camp"), P("camp"), P("camp"),
    )
    out_specs = (P("tm", None, "camp"), P("tm", None), P(None, "camp"), P("tm", "camp"))
    return jax.shard_map(shards, mesh=mesh, in_specs=in_specs, out_specs=out_specs, check_vma=False)
```

time: 212 us -> 67.7 us (0.32)
  blocking collectives: 123 us -> 0 us
  Pallas kernels: 0 us -> 55 us
  other arithmetic: 43.1 us -> 0 us
  waiting for transfers between devices: 17.9 us -> 0 us
  between operations: 14.4 us -> 0.66 us
    psum x2 -> x0, blocking collectives: 64.4 us -> none  [shards(): used = lax.psum(jnp.sum(share[None] * bar, axis=2), 'camp')]
    all_gather x4 -> x0, blocking collectives: 59 us -> none  [carried_in(): pieces = lax.all_gather(value, axis)]
    pallas_call x0 -> x1, Pallas kernels: none -> 55 us  [shards(): pl.pallas_call(kernel, out_shape=outs, in_specs=[anywhere, vmem, anywhere...]
    reduce_sum x4 -> x0, other arithmetic: 22.5 us -> none  [the longest x2 21.6 us: shards(): jnp.sum(per_slot, axis=0)]
    psum x2 -> x0, waiting for transfers between devices: 17.8 us -> none  [shards(): deliv = lax.psum(local_deliv, 'tm')]
    add x10 -> x0, other arithmetic: 17.4 us -> none  [the longest x6 17.4 us: blend(): return keep * (2.0 * fresh - older) + (1.0 - keep) * start]
    unnamed x24 -> x20, local copies, waits for them, and re-layouts: 2.08 us -> 11.6 us
    rev x5 -> x0, local copies, waits for them, and re-layouts: 7.01 us -> none  [the longest x3 6.47 us: shards(): rev_local = jnp.flip(jnp.cumsum(jnp.flip(pdual, 0), 0), 0)]
  transfers between devices with their start and end apart: 2 -> 0, of which waited for: 2 -> 0; matrix products, arithmetic and copies ran while one was open for 6% -> 0% of each run, Pallas kernels for 0% -> 0%
where the time goes in v1:
time: 67.7 us; the launch traced here: 67.3 us
  Pallas kernels  55 us (81%)
  local copies, waits for them, and re-layouts  11.6 us (17%)
    pallas_call x1, Pallas kernels, shards(): pl.pallas_call(kernel, out_shape=outs, in_specs=[anywhere, vmem, anywhere...  55 us
    unnamed x20, local copies, waits for them, and re-layouts  11.6 us

profile of v1, /device:TPU:1, one launch (start us, length us, event | category | flops | bytes accessed | tf_op | source)
XLA Modules:
  0.0 67.3 jit_solution(15540585410638582128)
XLA Ops:
  0.6 0.0 copy-start
  0.6 1.4 %copy-done = f32[192,2048]{1,0:T(8,128)S(1)} copy-done((f32[192,2048]{1,0:T(8,128)S(1)}, f32[192,2048]{1,0:T(8,128)}, u32[]{:S(2)}) %copy-start) | copy-done | bytes 1572888
  2.0 0.0 copy-start.1
  2.0 0.9 %copy-done.1 = s32[24,2048]{1,0:T(8,128)S(1)} copy-done((s32[24,2048]{1,0:T(8,128)S(1)}, s32[24,2048]{1,0:T(8,128)}, u32[]{:S(2)}) %copy-start.1) | copy-done | bytes 196632
  3.0 0.0 copy-start.2
  3.0 0.8 %copy-done.2 = f32[4,2048]{1,0:T(4,128)S(1)} copy-done((f32[4,2048]{1,0:T(4,128)S(1)}, f32[4,2048]{1,0:T(4,128)}, u32[]{:S(2)}) %copy-start.2) | copy-done | bytes 32792
  3.7 0.0 copy-start.3
  3.7 0.7 %copy-done.3 = f32[2048]{0:T(1024)S(1)} copy-done((f32[2048]{0:T(1024)S(1)}, f32[2048]{0:T(1024)}, u32[]{:S(2)}) %copy-start.3) | copy-done | bytes 8216
  4.4 0.0 copy-start.4
  4.4 0.7 %copy-done.4 = s32[2048]{0:T(1024)S(1)} copy-done((s32[2048]{0:T(1024)S(1)}, s32[2048]{0:T(1024)}, u32[]{:S(2)}) %copy-start.4) | copy-done | bytes 8216
  5.1 0.0 copy-start.5
  5.1 0.7 %copy-done.5 = s32[2048]{0:T(1024)S(1)} copy-done((s32[2048]{0:T(1024)S(1)}, s32[2048]{0:T(1024)}, u32[]{:S(2)}) %copy-start.5) | copy-done | bytes 8216
  5.8 0.0 copy-start.6
  5.8 0.7 %copy-done.6 = f32[4,192]{1,0:T(4,128)S(1)} copy-done((f32[4,192]{1,0:T(4,128)S(1)}, f32[4,192]{1,0:T(4,128)}, u32[]{:S(2)}) %copy-start.6) | copy-done | bytes 3096
  6.5 0.0 copy-start.7
  6.5 0.7 %copy-done.7 = f32[4,192]{1,0:T(4,128)S(1)} copy-done((f32[4,192]{1,0:T(4,128)S(1)}, f32[4,192]{1,0:T(4,128)}, u32[]{:S(2)}) %copy-start.7) | copy-done | bytes 3096
  7.2 55.0 %shard_map.156 = (f32[4,192,2048]{2,1,0:T(8,128)S(1)}, f32[4,192]{1,0:T(4,128)S(1)}, f32[192,2048]{1,0:T(8,128)S(1)}, f32[4,2048]{1,0:T(4,128)S(1)}) custom-call(f32[4,192,2048]{2,1,0:T(8,128)} %x0_hbm.1, f32[4,192]{1,0:T(4,128)S(1)} %copy-done.6, f32[192,2048]{1,0:T(8,128)S(1)} %copy-done, f32[4,2048]{1,0:T(4,128)S(1)} %copy-done.2, f32[192,2048]{1,0:T(8,128)} %value_hbm.1, ...), custom_call_target="tpu_custom_call" | custom-call | tf_op jit(solution)/shard_map/pallas_call | solution.py:440
  62.2 2.7 %copy.21 = f32[4,192,2048]{2,1,0:T(8,128)} copy(f32[4,192,2048]{2,1,0:T(8,128)S(1)} %get-tuple-element.4) | data formatting | bytes 12582912
  64.9 1.1 %copy.22 = f32[192,2048]{1,0:T(8,128)} copy(f32[192,2048]{1,0:T(8,128)S(1)} %get-tuple-element.6) | data formatting | bytes 3145728
  66.1 0.6 copy.23
  66.7 0.6 copy.24
Async XLA Ops:
  0.6 1.4 %copy-start = (f32[192,2048]{1,0:T(8,128)S(1)}, f32[192,2048]{1,0:T(8,128)}, u32[]{:S(2)}) copy-start(f32[192,2048]{1,0:T(8,128)} %r0_hbm.1) | copy-start | bytes 4718596
  2.0 0.9 %copy-start.1 = (s32[24,2048]{1,0:T(8,128)S(1)}, s32[24,2048]{1,0:T(8,128)}, u32[]{:S(2)}) copy-start(s32[24,2048]{1,0:T(8,128)} %elig_ref.1) | copy-start | bytes 589828
  3.0 0.8 %copy-start.2 = (f32[4,2048]{1,0:T(4,128)S(1)}, f32[4,2048]{1,0:T(4,128)}, u32[]{:S(2)}) copy-start(f32[4,2048]{1,0:T(4,128)} %p0_ref.1) | copy-start | bytes 98308
  3.7 0.7 %copy-start.3 = (f32[2048]{0:T(1024)S(1)}, f32[2048]{0:T(1024)}, u32[]{:S(2)}) copy-start(f32[2048]{0:T(1024)} %param.21) | copy-start | bytes 24580
  4.4 0.7 %copy-start.4 = (s32[2048]{0:T(1024)S(1)}, s32[2048]{0:T(1024)}, u32[]{:S(2)}) copy-start(s32[2048]{0:T(1024)} %param.24) | copy-start | bytes 24580
  5.1 0.7 %copy-start.5 = (s32[2048]{0:T(1024)S(1)}, s32[2048]{0:T(1024)}, u32[]{:S(2)}) copy-start(s32[2048]{0:T(1024)} %param.25) | copy-start | bytes 24580
  5.8 0.7 %copy-start.6 = (f32[4,192]{1,0:T(4,128)S(1)}, f32[4,192]{1,0:T(4,128)}, u32[]{:S(2)}) copy-start(f32[4,192]{1,0:T(4,128)} %s0_ref.1) | copy-start | bytes 9220
  6.5 0.7 %copy-start.7 = (f32[4,192]{1,0:T(4,128)S(1)}, f32[4,192]{1,0:T(4,128)}, u32[]{:S(2)}) copy-start(f32[4,192]{1,0:T(4,128)} %supply_ref.1) | copy-start | bytes 9220

commit v2 on v1

--- a/solution.py
+++ b/solution.py
@@ -29,9 +29,10 @@
 
 
 def kernel(
-    x0_hbm, s0_ref, r0_hbm, p0_ref, value_hbm, share_hbm, price_hbm, rcap_hbm,
-    limit_ref, supply_ref, elig_ref, begin_ref, span_ref,
+    x0_hbm, s0_hbm, r0_hbm, p0_hbm, value_hbm, share_hbm, price_hbm, rcap_hbm,
+    limit_hbm, supply_hbm, elig_hbm, begin_hbm, span_hbm,
     x_ref, s_out, r_ref, p_out,
+    s0_ref, p0_ref, limit_ref, supply_ref, elig_ref, begin_ref, span_ref,
     x0, value, share, price, r0, rcap,
     deliv, from_sib, from_x, r1,
     pen, sb, s8, s1, used, uz, uy,
@@ -62,6 +63,12 @@
         cp.start()
         loads.append(cp)
 
+    for src, dst in (
+        (p0_hbm, p0_ref), (s0_hbm, s0_ref), (elig_hbm, elig_ref), (begin_hbm, begin_ref),
+        (span_hbm, span_ref), (limit_hbm, limit_ref), (supply_hbm, supply_ref),
+    ):
+        load(src, dst)
+    small = len(loads)
     load(value_hbm, value)
     for t in range(NT):
         load(x0_hbm.at[t], x0.at[t])
@@ -74,6 +81,9 @@
     greet = tms + zs + ys
     for to in greet:
         pl.semaphore_signal(barrier, inc=1, device_id=to, device_id_type=MESH)
+
+    for cp in loads[:small]:
+        cp.wait()
 
     def spread_supply(rows):
         s8[0:NT, :] = rows * -0.5
@@ -99,7 +109,7 @@
         frac = jnp.clip((slot + 1 - begin).astype(jnp.float32) / span.astype(jnp.float32), 0.0, 1.0)
         cap[t] = limit_ref[...] * frac
     tstart[tm] = pk0[0] + pk0[1] + pk0[2] + pk0[3]
-    loads[0].wait()
+    loads[small].wait()
 
     def value_body(rb, carry):
         rows = pl.ds(pl.multiple_of(rb * 8, 8), 8)
@@ -137,7 +147,7 @@
         masked_total(lambda m: tstart[m], True),
         slice(0, NL),
     )
-    for cp in loads[1:]:
+    for cp in loads[small + 1 :]:
         cp.wait()
     used[...] = jnp.zeros_like(used)
 
@@ -387,6 +397,27 @@
         sibb_wait(1, i)
 
 
+def write_out(x, s, r, p, x_hbm, s_hbm, r_hbm, p_hbm, sem):
+    cps = []
+
+    def store(src, dst):
+        cp = pltpu.make_async_copy(src, dst, sem.at[len(cps)])
+        cp.start()
+        cps.append(cp)
+
+    for t in range(NT):
+        for h in range(2):
+            rows = pl.ds(h * (S // 2), S // 2)
+            store(x.at[t, rows], x_hbm.at[t, rows])
+    for h in range(2):
+        rows = pl.ds(h * (S // 2), S // 2)
+        store(r.at[rows], r_hbm.at[rows])
+    store(s, s_hbm)
+    store(p, p_hbm)
+    for cp in cps:
+        cp.wait()
+
+
 def shards(
     primal_start, supply_start, reach_start, spend_start, value, share, price, reach_cap,
     spend_limit, supply, eligible, start_slot, active_span,
@@ -397,11 +428,18 @@
     dma = pltpu.SemaphoreType.DMA
     outs = (
         pltpu.VMEM((NT, S, CD), f32),
-        jax.ShapeDtypeStruct((NT, S), f32),
+        pltpu.VMEM((NT, S), f32),
         pltpu.VMEM((S, CD), f32),
-        jax.ShapeDtypeStruct((NT, CD), f32),
+        pltpu.VMEM((NT, CD), f32),
     )
     scratch = [
+        pltpu.VMEM((NT, S), f32),
+        pltpu.VMEM((NT, CD), f32),
+        pltpu.VMEM((NL, 128), f32),
+        pltpu.VMEM((NT, S), f32),
+        pltpu.VMEM((S // SEG_BLOCK, CD), jnp.int32),
+        pltpu.VMEM((NL, 128), jnp.int32),
+        pltpu.VMEM((NL, 128), jnp.int32),
         pltpu.VMEM((NT, S, CD), f32),
         pltpu.VMEM((S, CD), f32),
         pltpu.VMEM((S, CD), f32),
@@ -427,7 +465,7 @@
         pltpu.VMEM((2, NT, NL, 128), f32),
         pltpu.VMEM((8, NL, 128), f32),
         pltpu.VMEM((3, NG, 8, GL, 128), f32),
-        dma((NT + 5,)),
+        dma((NT + 12,)),
         dma((2, NC)), dma((2, NC)),
         dma((2, NC, 3)), dma((2, NC, 3)),
         dma((2, NC, 3)), dma((2, NC, 3)),
@@ -437,21 +475,31 @@
         dma((2, 3)), dma((2, 3)),
         dma((2, 3)), dma((2, 3)),
     ]
+    args = (
+        primal_start, supply_start, reach_start, spend_start, value, share, price, reach_cap,
+        spend_limit.reshape(NL, 128), supply, eligible,
+        start_slot.reshape(NL, 128), active_span.reshape(NL, 128),
+    )
     res = pl.pallas_call(
         kernel,
         out_shape=outs,
-        in_specs=[anywhere, vmem, anywhere, vmem] + [anywhere] * 4 + [vmem] * 5,
-        out_specs=(vmem, vmem, vmem, vmem),
+        in_specs=[anywhere] * 13,
+        out_specs=(vmem,) * 4,
         scratch_shapes=scratch,
         compiler_params=pltpu.CompilerParams(
             collective_id=0, has_side_effects=True, vmem_limit_bytes=44 * 2**20
         ),
-    )(
-        primal_start, supply_start, reach_start, spend_start, value, share, price, reach_cap,
-        spend_limit.reshape(NL, 128), supply, eligible,
-        start_slot.reshape(NL, 128), active_span.reshape(NL, 128),
+    )(*[pltpu.with_memory_space_constraint(a, pltpu.HBM) for a in args])
+    return tuple(
+        pl.pallas_call(
+            write_out,
+            out_shape=tuple(pltpu.HBM(o.shape, o.dtype) for o in outs),
+            in_specs=[vmem] * 4,
+            out_specs=(anywhere,) * 4,
+            scratch_shapes=[dma((16,))],
+            compiler_params=pltpu.CompilerParams(vmem_limit_bytes=2**20),
+        )(*res)
     )
-    return tuple(res)
 
 
 def solution(mesh):

time: 67.7 us -> 59.2 us (0.87)
  local copies, waits for them, and re-layouts: 11.6 us -> 0 us
  Pallas kernels: 55 us -> 58.4 us
    unnamed x20 -> x0, local copies, waits for them, and re-layouts: 11.6 us -> none
    pallas_call x1 -> x2, Pallas kernels: 55 us -> 58.4 us  [the longest x1 55.1 us: shards(): pl.pallas_call(kernel, out_shape=outs, in_specs=[anywhere] * 13, out_spec...]
where the time goes in v2:
time: 59.2 us; the launch traced here: 59.1 us
  Pallas kernels  58.4 us (99%)
  between operations  0.64 us (1%)
    pallas_call x1, Pallas kernels, shards(): pl.pallas_call(kernel, out_shape=outs, in_specs=[anywhere] * 13, out_spec...  55.1 us
    pallas_call x1, Pallas kernels, shards(): pl.pallas_call(write_out, out_shape=tuple((pltpu.HBM(o.shape, o.dtype) fo...  3.29 us

profile of v2, /device:TPU:1, one launch (start us, length us, event | category | flops | bytes accessed | tf_op | source)
XLA Modules:
  0.0 59.1 jit_solution(5066426669128869749)
XLA Ops:
  0.6 55.1 %shard_map.156 = (f32[4,192,2048]{2,1,0:T(8,128)S(1)}, f32[4,192]{1,0:T(4,128)S(1)}, f32[192,2048]{1,0:T(8,128)S(1)}, f32[4,2048]{1,0:T(4,128)S(1)}) custom-call(f32[4,192,2048]{2,1,0:T(8,128)} %x0_hbm.1, f32[4,192]{1,0:T(4,128)} %s0_hbm.1, f32[192,2048]{1,0:T(8,128)} %r0_hbm.1, f32[4,2048]{1,0:T(4,128)} %p0_hbm.1, f32[192,2048]{1,0:T(8,128)} %value_hbm.1, ...), custom_call_target="tpu_custom_call" | custom-call | tf_op jit(solution)/shard_map/pallas_call | solution.py:483
  55.8 3.3 %shard_map.157 = (f32[4,192,2048]{2,1,0:T(8,128)}, f32[4,192]{1,0:T(4,128)}, f32[192,2048]{1,0:T(8,128)}, f32[4,2048]{1,0:T(4,128)}) custom-call(f32[4,192,2048]{2,1,0:T(8,128)S(1)} %get-tuple-element.8.x, f32[4,192]{1,0:T(4,128)S(1)} %get-tuple-element.9.s, f32[192,2048]{1,0:T(8,128)S(1)} %get-tuple-element.10.r, f32[4,2048]{1,0:T(4,128)S(1)} %get-tuple-element.11.p), custom_call_target="tpu_custom_call" | custom-call | tf_op jit(solution)/shard_map/pallas_call | solution.py:494

commit v3 on v2

--- a/solution.py
+++ b/solution.py
@@ -15,9 +15,12 @@
 NT = 4
 CD = 2048
 NL = CD // 128
-LT = 2
+HL = 1
+LT = 2 * HL
+HW = HL * 128
 NC = NL // LT
 QR = S // 4
+HR = QR // 2
 NG = 2
 GL = NL // NG
 GC = NC // NG
@@ -26,6 +29,52 @@
 SIG_SUPPLY = 4.0 / CAMPAIGNS
 SIG_REACH = 1.0 / (2 * SLOTS)
 SIG_SPEND = 1.0 / (S * SLOTS * SLOTS)
+
+
+RS_RING = ((1,) * NC, (1,) * NC)
+AG_RING = ((1,) * NC, (1,) * NC)
+
+
+def make_order():
+    o = []
+    for i in range(NC):
+        o.append(("comp", 0, i))
+        if i >= 3:
+            o.append(("rs1", 0, i - 3))
+        if i == GC - 1:
+            o.append(("sp1", 0, 0))
+    o += [("uz", 0), ("sp1", 0, 1), ("rs1", 0, 5), ("rs1", 0, 6), ("rs1", 0, 7), ("caps",)]
+    o += [("rs2", 0, 0), ("rs2", 0, 1), ("rs2", 0, 2), ("sp2", 0, 0)]
+    o += [("rs2", 0, i) for i in range(3, 8)]
+    o += [("uy", 0), ("ag1", 0, 0), ("ag1", 0, 1), ("sp2", 0, 1)]
+    o += [("ag1", 0, i) for i in range(2, 8)]
+    o += [("sp3", 0), ("ag2", 0, 0), ("ag2", 0, 1), ("ue", 0)]
+    o += [("ag2", 0, i) for i in range(2, 6)]
+    o += [("sibb", 0, 0), ("sibb", 0, 1), ("ag2", 0, 6), ("ag2", 0, 7), ("sp3", 1)]
+    for i in range(NC):
+        o.append(("fin", 0, i))
+        o.append(("comp", 1, i))
+        if i + 2 < NC:
+            o.append(("sibb", 0, i + 2))
+        if i >= 2:
+            o.append(("rs1", 1, i - 2))
+        if i == GC - 1:
+            o.append(("sp1", 1, 0))
+        if i >= 5:
+            o.append(("rs2", 1, i - 5))
+    o += [("rs1", 1, 6), ("rs1", 1, 7), ("uz", 1), ("sp1", 1, 1)]
+    o += [("rs2", 1, i) for i in range(3, 8)]
+    o += [("sp2", 1, 0)]
+    o += [("ag1", 1, i) for i in range(0, 8)]
+    o += [("uy", 1)]
+    o += [("ag2", 1, i) for i in range(0, 8)]
+    o += [("sp2", 1, 1), ("sibb", 1, 0), ("sibb", 1, 1), ("ue", 1)]
+    o += [("sibb", 1, i) for i in range(2, 8)]
+    o += [("fin", 1, i) for i in range(8)]
+    return o
+
+
+ORDER = make_order()
 
 
 def kernel(
@@ -34,11 +83,10 @@
     x_ref, s_out, r_ref, p_out,
     s0_ref, p0_ref, limit_ref, supply_ref, elig_ref, begin_ref, span_ref,
     x0, value, share, price, r0, rcap,
-    deliv, from_sib, from_x, r1,
+    deliv, from_sib, ring, from_x, r1,
     pen, sb, s8, s1, used, uz, uy,
     pk0, pk1, cap, live, zeff, spent, tstart, tots,
-    ld, siba_s, siba_r, rs_s, rs_r, ag_s, ag_r, sibb_s, sibb_r,
-    t0_s, t0_r, tot_s, tot_r, uz_s, uz_r, uy_s, uy_r,
+    ld, sent, siba_r, rs1_r, rs2_r, ag1_r, ag2_r, sibb_r, t0_s, t0_r, tot_s, tot_r, used_s, used_r,
 ):
     camp = lax.axis_index("camp")
     tm = lax.axis_index("tm")
@@ -49,12 +97,21 @@
     tms = [(camp, (tm + d) % 8) for d in range(1, 8)]
     zs = [(y * 4 + (z + d) % 4, tm) for d in (1, 2, 3)]
     ys = [(((y + d) % 4) * 4 + z, tm) for d in (1, 2, 3)]
+    right, left = xs[0], xs[2]
     mine = pl.multiple_of(x * QR, 8)
+
+    def wait_for(like, sem):
+        pltpu.make_async_copy(like, like, sem).wait()
 
     def send(src, dst, ssem, rsem, to):
         return pltpu.make_async_remote_copy(
             src_ref=src, dst_ref=dst, send_sem=ssem, recv_sem=rsem, device_id=to, device_id_type=MESH
         )
+
+    barrier = pltpu.get_barrier_semaphore()
+    greet = tms + zs + ys
+    for to in greet:
+        pl.semaphore_signal(barrier, inc=1, device_id=to, device_id_type=MESH)
 
     loads = []
 
@@ -77,13 +134,12 @@
     load(r0_hbm, r0)
     load(rcap_hbm.at[pl.ds(mine, QR)], rcap)
 
-    barrier = pltpu.get_barrier_semaphore()
-    greet = tms + zs + ys
-    for to in greet:
-        pl.semaphore_signal(barrier, inc=1, device_id=to, device_id_type=MESH)
-
     for cp in loads[:small]:
         cp.wait()
+    for t in range(NT):
+        for lt in range(NL):
+            pk0[t, lt : lt + 1, :] = p0_ref[t : t + 1, lt * 128 : (lt + 1) * 128]
+    tstart[tm] = pk0[0] + pk0[1] + pk0[2] + pk0[3]
 
     def spread_supply(rows):
         s8[0:NT, :] = rows * -0.5
@@ -94,21 +150,24 @@
                 table, pick, (((0,), (0,)), ((), ())), precision=HIGHEST, preferred_element_type=jnp.float32
             )
 
-    s8[...] = jnp.zeros_like(s8)
-    spread_supply(s0_ref[...])
-    for b in range(S // SEG_BLOCK):
-        pen[b] = jnp.where(elig_ref[b : b + 1, :] > 0, 0.0, BLOCKED)
-    for t in range(NT):
-        for lt in range(NL):
-            pk0[t, lt : lt + 1, :] = p0_ref[t : t + 1, lt * 128 : (lt + 1) * 128]
     begin = begin_ref[...]
     span = span_ref[...]
     for t in range(NT):
         slot = tm * NT + t
         live[t] = ((slot >= begin) & (slot < begin + span)).astype(jnp.float32)
-        frac = jnp.clip((slot + 1 - begin).astype(jnp.float32) / span.astype(jnp.float32), 0.0, 1.0)
-        cap[t] = limit_ref[...] * frac
-    tstart[tm] = pk0[0] + pk0[1] + pk0[2] + pk0[3]
+
+    pl.semaphore_wait(barrier, len(greet))
+
+    cps = [
+        send(tstart.at[tm], tstart.at[tm], t0_s.at[0], t0_r.at[0], tms[d]) for d in range(7)
+    ]
+    for cp in cps:
+        cp.start()
+
+    s8[...] = jnp.zeros_like(s8)
+    spread_supply(s0_ref[...])
+    for b in range(S // SEG_BLOCK):
+        pen[b] = jnp.where(elig_ref[b : b + 1, :] > 0, 0.0, BLOCKED)
     loads[small].wait()
 
     def value_body(rb, carry):
@@ -117,14 +176,9 @@
         return carry
 
     lax.fori_loop(0, S // 8, value_body, 0)
-
-    pl.semaphore_wait(barrier, len(greet))
-
-    cps = [
-        send(tstart.at[tm], tstart.at[tm], t0_s.at[d], t0_r.at[d], tms[d]) for d in range(7)
-    ]
-    for cp in cps:
-        cp.start()
+    used[...] = jnp.zeros_like(used)
+    for cp in loads[small + 1 :]:
+        cp.wait()
 
     def masked_total(parts, later):
         total = None
@@ -140,16 +194,13 @@
             run = run + duals[t]
             zeff[t, rows, :] = jnp.where(live[t, rows, :] > 0.0, -0.5 * run, BLOCKED)
 
-    for cp in cps:
-        cp.wait()
+    wait_for(tstart.at[pl.ds(0, 7)], t0_s.at[0])
+    wait_for(tstart.at[pl.ds(0, 7)], t0_r.at[0])
     set_zeff(
         [pk0[t] for t in range(NT)],
         masked_total(lambda m: tstart[m], True),
         slice(0, NL),
     )
-    for cp in loads[small + 1 :]:
-        cp.wait()
-    used[...] = jnp.zeros_like(used)
 
     def comp(it, i):
         zb = [
@@ -165,7 +216,7 @@
                 cols = pl.ds((i * LT + l) * 128, 128)
                 sh = share[rows, cols]
                 pr = price[rows, cols]
-                rd = r0[rows, cols] if it == 0 else r1[i, l, rows, :]
+                rd = r0[rows, cols] if it == 0 else r1[rows, cols]
                 base = value[rows, cols] - 0.5 * rd
                 total = None
                 for t in range(NT):
@@ -180,7 +231,7 @@
                         x_ref[t, rows, cols] = new
                     else:
                         x_ref[t, rows, cols] = (2.0 / 3.0) * bar + (1.0 / 3.0) * x0[t, rows, cols]
-                deliv[it, i, l, rows, :] = total
+                deliv[it, rows, cols] = total
             for t in range(NT):
                 used[t, rows, :] = used[t, rows, :] + uses[t]
             return tuple(acc)
@@ -191,67 +242,91 @@
             for l in range(LT):
                 spent[it, t, i * LT + l : i * LT + l + 1, :] = jnp.sum(acc[t * LT + l], axis=0, keepdims=True)
 
-    pend = {}
-
-    def siba_start(it, i):
-        cp = send(deliv.at[it, i, 1 - core], from_sib.at[it, i], siba_s.at[it, i], siba_r.at[it, i], sib)
-        cp.start()
-        pend["a", it, i] = cp
-
-    def rs_start(it, i):
-        pend["a", it, i].wait()
-        deliv[it, i, core] = deliv[it, i, core] + from_sib[it, i]
-        cps = []
-        for d in (1, 2, 3):
-            theirs = pl.multiple_of(((x + d) % 4) * QR, 8)
-            cps.append(
-                send(
-                    deliv.at[it, i, core, pl.ds(theirs, QR)],
-                    from_x.at[it, i, d - 1],
-                    rs_s.at[it, i, d - 1],
-                    rs_r.at[it, i, d - 1],
-                    xs[d - 1],
-                )
-            )
-        for cp in cps:
-            cp.start()
-        pend["rs", it, i] = cps
-
-    def out_cols(i, half):
-        return pl.ds(pl.multiple_of((i * LT + half) * 128, 128), 128)
-
-    def ag_start(it, i):
-        for cp in pend["rs", it, i]:
-            cp.wait()
-        rows = pl.ds(mine, QR)
-        cols = out_cols(i, core)
-        total = deliv[it, i, core, rows, :] + from_x[it, i, 0] + from_x[it, i, 1] + from_x[it, i, 2]
+    def half(i, core_of):
+        return pl.ds(pl.multiple_of((i * LT + core_of * HL) * 128, 128), HW)
+
+    def part(chip, first, rows):
+        return pl.ds(pl.multiple_of(chip * QR + first, 8), rows)
+
+    opposite, after, before = (x + 2) % 4, (x + 1) % 4, (x + 3) % 4
+    whole_half = from_sib.at[0, :, pl.ds(0, HW)]
+
+    def two(buf, rows, n=2):
+        return buf.at[0, pl.ds(0, n), pl.ds(0, rows), pl.ds(0, HW)]
+
+    def go(it, i, src, dst, rsem, to):
+        send(src, dst, sent.at[it, i], rsem.at[i], to).start()
+
+    def siba(it, i):
+        cols = half(i, 1 - core)
+        go(it, i, deliv.at[it, :, cols], from_sib.at[it, :, cols], siba_r, sib)
+
+    def rs1(it, i):
+        cols = half(i, core)
+        wait_for(whole_half, siba_r.at[i])
+        deliv[it, :, cols] = deliv[it, :, cols] + from_sib[it, :, cols]
+        if RS_RING[it][i]:
+            go(it, i, deliv.at[it, part(opposite, 0, HR), cols], ring.at[it, 0, :, cols], rs1_r, right)
+            go(it, i, deliv.at[it, part(opposite, HR, HR), cols], ring.at[it, 1, :, cols], rs1_r, left)
+        else:
+            for d, chip, to in ((0, after, xs[0]), (1, before, xs[2]), (2, opposite, xs[1])):
+                go(it, i, deliv.at[it, part(chip, 0, QR), cols], from_x.at[it, d, :, cols], rs2_r, to)
+
+    def rs2(it, i):
+        if RS_RING[it][i]:
+            cols = half(i, core)
+            wait_for(two(ring, HR), rs1_r.at[i])
+            rows = part(after, 0, HR)
+            deliv[it, rows, cols] = deliv[it, rows, cols] + ring[it, 0, :, cols]
+            rows = part(before, HR, HR)
+            deliv[it, rows, cols] = deliv[it, rows, cols] + ring[it, 1, :, cols]
+            go(it, i, deliv.at[it, part(after, 0, QR), cols], from_x.at[it, 0, :, cols], rs2_r, right)
+            go(it, i, deliv.at[it, part(before, 0, QR), cols], from_x.at[it, 1, :, cols], rs2_r, left)
+
+    def ag1(it, i):
+        cols = half(i, core)
+        rows = part(x, 0, QR)
+        wait_for(two(from_x, QR, 2 if RS_RING[it][i] else 3), rs2_r.at[i])
+        total = deliv[it, rows, cols] + from_x[it, 0, :, cols] + from_x[it, 1, :, cols]
+        if not RS_RING[it][i]:
+            total = total + from_x[it, 2, :, cols]
         start = r0[rows, cols]
         if it == 0:
-            r1[i, core, rows, :] = jnp.maximum(start + SIG_REACH * (total - rcap[:, cols]), 0.0)
-            piece = r1.at[i, core, rows]
+            r1[rows, cols] = jnp.maximum(start + SIG_REACH * (total - rcap[:, cols]), 0.0)
         else:
-            old = r1[i, core, rows, :]
+            old = r1[rows, cols]
             new = jnp.maximum(old + SIG_REACH * (total - rcap[:, cols]), 0.0)
             r_ref[rows, cols] = (2.0 / 3.0) * (2.0 * new - old) + (1.0 / 3.0) * start
-            piece = r_ref.at[rows, cols]
-        cps = [
-            send(piece, piece, ag_s.at[it, i, d], ag_r.at[it, i, d], xs[d]) for d in range(3)
-        ]
-        for cp in cps:
-            cp.start()
-        pend["ag", it, i] = cps
-
-    def sibb_start(it, i):
-        for cp in pend["ag", it, i]:
-            cp.wait()
-        piece = r1.at[i, core] if it == 0 else r_ref.at[:, out_cols(i, core)]
-        cp = send(piece, piece, sibb_s.at[it, i], sibb_r.at[it, i], sib)
-        cp.start()
-        pend["b", it, i] = cp
-
-    def sibb_wait(it, i):
-        pend["b", it, i].wait()
+        piece = (r1 if it == 0 else r_ref).at[rows, cols]
+        go(it, i, piece, piece, ag1_r, right)
+        go(it, i, piece, piece, ag1_r, left)
+        if not AG_RING[it][i]:
+            go(it, i, piece, piece, ag1_r, xs[1])
+
+    def ag2(it, i):
+        wait_for(two(from_x, QR, 2 if AG_RING[it][i] else 3), ag1_r.at[i])
+        if AG_RING[it][i]:
+            cols = half(i, core)
+            out = r1 if it == 0 else r_ref
+            piece = out.at[part(before, 0, HR), cols]
+            go(it, i, piece, piece, ag2_r, right)
+            piece = out.at[part(after, HR, HR), cols]
+            go(it, i, piece, piece, ag2_r, left)
+
+    def sibb(it, i):
+        if AG_RING[it][i]:
+            wait_for(two(ring, HR), ag2_r.at[i])
+        out = r1 if it == 0 else r_ref
+        piece = out.at[:, half(i, core)]
+        go(it, i, piece, piece, sibb_r, sib)
+
+    def fin(it, i):
+        wait_for(whole_half, sibb_r.at[i])
+
+    def all_sent():
+        for it in range(2):
+            for i in range(NC):
+                wait_for(x0.at[0, pl.ds(0, 168), pl.ds(0, 4 * HW)], sent.at[it, i])
 
     def used_z(it):
         total = None
@@ -264,23 +339,19 @@
             term = jnp.where(row, term, 0.0)
             total = term if total is None else total + term
         uz[it, z] = total
-        cps = [send(uz.at[it, z], uz.at[it, z], uz_s.at[it, d], uz_r.at[it, d], zs[d]) for d in range(3)]
-        for cp in cps:
-            cp.start()
-        pend["uz", it] = cps
+        for to in zs:
+            send(uz.at[it, z], uz.at[it, z], used_s.at[it, 0], used_r.at[it, 0], to).start()
 
     def used_y(it):
-        for cp in pend["uz", it]:
-            cp.wait()
+        for sem in (used_s, used_r):
+            wait_for(uz.at[it, pl.ds(0, 3)], sem.at[it, 0])
         uy[it, y] = uz[it, 0] + uz[it, 1] + uz[it, 2] + uz[it, 3]
-        cps = [send(uy.at[it, y], uy.at[it, y], uy_s.at[it, d], uy_r.at[it, d], ys[d]) for d in range(3)]
-        for cp in cps:
-            cp.start()
-        pend["uy", it] = cps
+        for to in ys:
+            send(uy.at[it, y], uy.at[it, y], used_s.at[it, 1], used_r.at[it, 1], to).start()
 
     def used_end(it):
-        for cp in pend["uy", it]:
-            cp.wait()
+        for sem in (used_s, used_r):
+            wait_for(uy.at[it, pl.ds(0, 3)], sem.at[it, 1])
         total = uy[it, 0] + uy[it, 1] + uy[it, 2] + uy[it, 3]
         total = total[0:NT, :]
         if it == 0:
@@ -294,17 +365,12 @@
 
     def share_total(e, g, value):
         tots[e, g, tm] = value
-        cps = [
-            send(tots.at[e, g, tm], tots.at[e, g, tm], tot_s.at[e, g, d], tot_r.at[e, g, d], tms[d])
-            for d in range(7)
-        ]
-        for cp in cps:
-            cp.start()
-        pend["t", e, g] = cps
+        for to in tms:
+            send(tots.at[e, g, tm], tots.at[e, g, tm], tot_s.at[e, g], tot_r.at[e, g], to).start()
 
     def wait_total(e, g, later):
-        for cp in pend["t", e, g]:
-            cp.wait()
+        for sem in (tot_s, tot_r):
+            wait_for(tots.at[e, g, pl.ds(0, 7)], sem.at[e, g])
         return masked_total(lambda m: tots[e, g, m], later)
 
     def spend_1(it, g):
@@ -335,66 +401,27 @@
         later = wait_total(1, g, True)
         set_zeff([pk1[t, rows] for t in range(NT)], later, rows)
 
-    for i in range(NC):
-        comp(0, i)
-        siba_start(0, i)
-        if i >= 1:
-            rs_start(0, i - 1)
-        if i == GC - 1:
-            spend_1(0, 0)
-    used_z(0)
-    spend_1(0, 1)
-    rs_start(0, NC - 1)
-    for i in range(0, 2):
-        ag_start(0, i)
-    spend_2(0, 0)
-    for i in range(2, 4):
-        ag_start(0, i)
-    used_y(0)
-    spend_2(0, 1)
-    for i in range(4, 6):
-        ag_start(0, i)
-    sibb_start(0, 0)
-    spend_3(0)
-    ag_start(0, 6)
-    sibb_start(0, 1)
-    used_end(0)
-    used[...] = jnp.zeros_like(used)
-    ag_start(0, 7)
-    for i in range(NC):
-        sibb_wait(0, i)
-        if i + 2 < NC:
-            sibb_start(0, i + 2)
-        if i == GC:
-            spend_3(1)
-        comp(1, i)
-        siba_start(1, i)
-        if i >= 1:
-            rs_start(1, i - 1)
-        if i >= 4:
-            ag_start(1, i - 4)
-        if i == GC - 1:
-            spend_1(1, 0)
-    used_z(1)
-    spend_1(1, 1)
-    rs_start(1, NC - 1)
-    sibb_start(1, 0)
-    ag_start(1, 4)
-    sibb_start(1, 1)
-    ag_start(1, 5)
-    sibb_start(1, 2)
-    used_y(1)
-    spend_2(1, 0)
-    ag_start(1, 6)
-    sibb_start(1, 3)
-    spend_2(1, 1)
-    ag_start(1, 7)
-    sibb_start(1, 4)
-    used_end(1)
-    for i in range(5, NC):
-        sibb_start(1, i)
-    for i in range(NC):
-        sibb_wait(1, i)
+    def caps():
+        for t in range(NT):
+            frac = jnp.clip((tm * NT + t + 1 - begin).astype(jnp.float32) / span.astype(jnp.float32), 0.0, 1.0)
+            cap[t] = limit_ref[...] * frac
+
+    def new_supply(it):
+        used_end(it)
+        if it == 0:
+            used[...] = jnp.zeros_like(used)
+
+    def chunk(it, i):
+        comp(it, i)
+        siba(it, i)
+
+    steps = dict(
+        comp=chunk, rs1=rs1, rs2=rs2, ag1=ag1, ag2=ag2, sibb=sibb, fin=fin, uz=used_z, uy=used_y,
+        ue=new_supply, sp1=spend_1, sp2=spend_2, sp3=spend_3, caps=caps,
+    )
+    for name, *where in ORDER:
+        steps[name](*where)
+    all_sent()
 
 
 def write_out(x, s, r, p, x_hbm, s_hbm, r_hbm, p_hbm, sem):
@@ -446,10 +473,11 @@
         pltpu.VMEM((S, CD), f32),
         pltpu.VMEM((S, CD), f32),
         pltpu.VMEM((QR, CD), f32),
-        pltpu.VMEM((2, NC, LT, S, 128), f32),
-        pltpu.VMEM((2, NC, S, 128), f32),
-        pltpu.VMEM((2, NC, 3, QR, 128), f32),
-        pltpu.VMEM((NC, LT, S, 128), f32),
+        pltpu.VMEM((2, S, CD), f32),
+        pltpu.VMEM((2, S, CD), f32),
+        pltpu.VMEM((2, 2, HR, CD), f32),
+        pltpu.VMEM((2, 3, QR, CD), f32),
+        pltpu.VMEM((S, CD), f32),
         pltpu.VMEM((S // SEG_BLOCK, 1, CD), f32),
         pltpu.VMEM((NT, S, 128), f32),
         pltpu.VMEM((8, S), f32),
@@ -466,14 +494,11 @@
         pltpu.VMEM((8, NL, 128), f32),
         pltpu.VMEM((3, NG, 8, GL, 128), f32),
         dma((NT + 12,)),
-        dma((2, NC)), dma((2, NC)),
-        dma((2, NC, 3)), dma((2, NC, 3)),
-        dma((2, NC, 3)), dma((2, NC, 3)),
-        dma((2, NC)), dma((2, NC)),
-        dma((7,)), dma((7,)),
-        dma((3, NG, 7)), dma((3, NG, 7)),
-        dma((2, 3)), dma((2, 3)),
-        dma((2, 3)), dma((2, 3)),
+        dma((2, NC)),
+        dma((NC,)), dma((NC,)), dma((NC,)), dma((NC,)), dma((NC,)), dma((NC,)),
+        dma((1,)), dma((1,)),
+        dma((3, NG)), dma((3, NG)),
+        dma((2, 2)), dma((2, 2)),
     ]
     args = (
         primal_start, supply_start, reach_start, spend_start, value, share, price, reach_cap,

time: 59.2 us -> 57.3 us (0.968)
  Pallas kernels: 58.4 us -> 56.5 us
    pallas_call x1, Pallas kernels: 55.1 us -> 53.2 us  [shards(): pl.pallas_call(kernel, out_shape=outs, in_specs=[anywhere] * 13, out_spec...]
where the time goes in v3:
time: 57.3 us; the launch traced here: 57.2 us
  Pallas kernels  56.5 us (99%)
  between operations  0.64 us (1%)
    pallas_call x1, Pallas kernels, shards(): pl.pallas_call(kernel, out_shape=outs, in_specs=[anywhere] * 13, out_spec...  53.2 us
    pallas_call x1, Pallas kernels, shards(): pl.pallas_call(write_out, out_shape=tuple((pltpu.HBM(o.shape, o.dtype) fo...  3.29 us

profile of v3, /device:TPU:1, one launch (start us, length us, event | category | flops | bytes accessed | tf_op | source)
XLA Modules:
  0.0 57.2 jit_solution(12791770132114484190)
XLA Ops:
  0.6 53.2 %shard_map.156 = (f32[4,192,2048]{2,1,0:T(8,128)S(1)}, f32[4,192]{1,0:T(4,128)S(1)}, f32[192,2048]{1,0:T(8,128)S(1)}, f32[4,2048]{1,0:T(4,128)S(1)}) custom-call(f32[4,192,2048]{2,1,0:T(8,128)} %x0_hbm.1, f32[4,192]{1,0:T(4,128)} %s0_hbm.1, f32[192,2048]{1,0:T(8,128)} %r0_hbm.1, f32[4,2048]{1,0:T(4,128)} %p0_hbm.1, f32[192,2048]{1,0:T(8,128)} %value_hbm.1, ...), custom_call_target="tpu_custom_call" | custom-call | tf_op jit(solution)/shard_map/pallas_call | solution.py:508
  53.9 3.3 %shard_map.157 = (f32[4,192,2048]{2,1,0:T(8,128)}, f32[4,192]{1,0:T(4,128)}, f32[192,2048]{1,0:T(8,128)}, f32[4,2048]{1,0:T(4,128)}) custom-call(f32[4,192,2048]{2,1,0:T(8,128)S(1)} %get-tuple-element.8.x, f32[4,192]{1,0:T(4,128)S(1)} %get-tuple-element.9.s, f32[192,2048]{1,0:T(8,128)S(1)} %get-tuple-element.10.r, f32[4,2048]{1,0:T(4,128)S(1)} %get-tuple-element.11.p), custom_call_target="tpu_custom_call" | custom-call | tf_op jit(solution)/shard_map/pallas_call | solution.py:519

commit v4 on v3

--- a/solution.py
+++ b/solution.py
@@ -31,50 +31,27 @@
 SIG_SPEND = 1.0 / (S * SLOTS * SLOTS)
 
 
-RS_RING = ((1,) * NC, (1,) * NC)
-AG_RING = ((1,) * NC, (1,) * NC)
-
-
-def make_order():
-    o = []
-    for i in range(NC):
-        o.append(("comp", 0, i))
-        if i >= 3:
-            o.append(("rs1", 0, i - 3))
-        if i == GC - 1:
-            o.append(("sp1", 0, 0))
-    o += [("uz", 0), ("sp1", 0, 1), ("rs1", 0, 5), ("rs1", 0, 6), ("rs1", 0, 7), ("caps",)]
-    o += [("rs2", 0, 0), ("rs2", 0, 1), ("rs2", 0, 2), ("sp2", 0, 0)]
-    o += [("rs2", 0, i) for i in range(3, 8)]
-    o += [("uy", 0), ("ag1", 0, 0), ("ag1", 0, 1), ("sp2", 0, 1)]
-    o += [("ag1", 0, i) for i in range(2, 8)]
-    o += [("sp3", 0), ("ag2", 0, 0), ("ag2", 0, 1), ("ue", 0)]
-    o += [("ag2", 0, i) for i in range(2, 6)]
-    o += [("sibb", 0, 0), ("sibb", 0, 1), ("ag2", 0, 6), ("ag2", 0, 7), ("sp3", 1)]
-    for i in range(NC):
-        o.append(("fin", 0, i))
-        o.append(("comp", 1, i))
-        if i + 2 < NC:
-            o.append(("sibb", 0, i + 2))
-        if i >= 2:
-            o.append(("rs1", 1, i - 2))
-        if i == GC - 1:
-            o.append(("sp1", 1, 0))
-        if i >= 5:
-            o.append(("rs2", 1, i - 5))
-    o += [("rs1", 1, 6), ("rs1", 1, 7), ("uz", 1), ("sp1", 1, 1)]
-    o += [("rs2", 1, i) for i in range(3, 8)]
-    o += [("sp2", 1, 0)]
-    o += [("ag1", 1, i) for i in range(0, 8)]
-    o += [("uy", 1)]
-    o += [("ag2", 1, i) for i in range(0, 8)]
-    o += [("sp2", 1, 1), ("sibb", 1, 0), ("sibb", 1, 1), ("ue", 1)]
-    o += [("sibb", 1, i) for i in range(2, 8)]
-    o += [("fin", 1, i) for i in range(8)]
-    return o
-
-
-ORDER = make_order()
+RS_RING = ((1, 1, 1, 1, 1, 1, 0, 0), (0, 0, 0, 0, 0, 0, 0, 1))
+AG_RING = ((1, 0, 0, 0, 0, 0, 0, 1), (0, 1, 1, 1, 0, 1, 1, 1))
+ORDER = (
+    ("comp", 0, 5), ("comp", 0, 6), ("comp", 0, 7), ("comp", 0, 4), ("rs1", 0, 5), ("sp1", 0, 1),
+    ("comp", 0, 1), ("rs1", 0, 6), ("rs1", 0, 7), ("caps",), ("comp", 0, 0), ("comp", 0, 3), ("comp", 0, 2),
+    ("rs1", 0, 1), ("uz", 0), ("rs1", 0, 4), ("rs1", 0, 2), ("rs1", 0, 3), ("rs1", 0, 0), ("rs2", 0, 5),
+    ("sp2", 0, 1), ("sp1", 0, 0), ("ag1", 0, 6), ("ag1", 0, 7), ("rs2", 0, 1), ("rs2", 0, 3), ("ag1", 0, 5),
+    ("uy", 0), ("rs2", 0, 0), ("rs2", 0, 2), ("rs2", 0, 4), ("ag2", 0, 7), ("sibb", 0, 6), ("ag1", 0, 1),
+    ("fin", 0, 6), ("ag1", 0, 3), ("sibb", 0, 5), ("sp2", 0, 0), ("sp3", 1), ("ue", 0), ("ag1", 0, 0),
+    ("comp", 1, 6), ("ag1", 0, 2), ("fin", 0, 5), ("sibb", 0, 7), ("comp", 1, 5), ("ag1", 0, 4),
+    ("rs1", 1, 5), ("rs1", 1, 6), ("sibb", 0, 1), ("fin", 0, 7), ("comp", 1, 7), ("sibb", 0, 3), ("sp3", 0),
+    ("fin", 0, 1), ("comp", 1, 1), ("ag2", 0, 0), ("fin", 0, 3), ("comp", 1, 3), ("rs1", 1, 7),
+    ("sibb", 0, 2), ("rs1", 1, 1), ("rs1", 1, 3), ("sibb", 0, 4), ("fin", 0, 2), ("comp", 1, 2),
+    ("ag1", 1, 5), ("fin", 0, 4), ("comp", 1, 4), ("rs1", 1, 2), ("sibb", 0, 0), ("rs2", 1, 7), ("rs1", 1, 4),
+    ("fin", 0, 0), ("comp", 1, 0), ("ag1", 1, 1), ("uz", 1), ("rs1", 1, 0), ("ag1", 1, 3), ("ag1", 1, 2),
+    ("ag1", 1, 7), ("ag1", 1, 6), ("ag2", 1, 5), ("uy", 1), ("ag2", 1, 1), ("ag1", 1, 4), ("ag1", 1, 0),
+    ("ag2", 1, 2), ("ag2", 1, 3), ("ag2", 1, 7), ("ue", 1), ("ag2", 1, 6), ("sp1", 1, 1), ("sibb", 1, 5),
+    ("sp1", 1, 0), ("sibb", 1, 1), ("fin", 1, 5), ("fin", 1, 1), ("sibb", 1, 4), ("sibb", 1, 0),
+    ("sibb", 1, 2), ("sibb", 1, 3), ("fin", 1, 4), ("sibb", 1, 7), ("sibb", 1, 6), ("fin", 1, 0),
+    ("fin", 1, 2), ("fin", 1, 7), ("fin", 1, 3), ("sp2", 1, 1), ("sp2", 1, 0), ("fin", 1, 6),
+)
 
 
 def kernel(
@@ -273,15 +250,14 @@
                 go(it, i, deliv.at[it, part(chip, 0, QR), cols], from_x.at[it, d, :, cols], rs2_r, to)
 
     def rs2(it, i):
-        if RS_RING[it][i]:
-            cols = half(i, core)
-            wait_for(two(ring, HR), rs1_r.at[i])
-            rows = part(after, 0, HR)
-            deliv[it, rows, cols] = deliv[it, rows, cols] + ring[it, 0, :, cols]
-            rows = part(before, HR, HR)
-            deliv[it, rows, cols] = deliv[it, rows, cols] + ring[it, 1, :, cols]
-            go(it, i, deliv.at[it, part(after, 0, QR), cols], from_x.at[it, 0, :, cols], rs2_r, right)
-            go(it, i, deliv.at[it, part(before, 0, QR), cols], from_x.at[it, 1, :, cols], rs2_r, left)
+        cols = half(i, core)
+        wait_for(two(ring, HR), rs1_r.at[i])
+        rows = part(after, 0, HR)
+        deliv[it, rows, cols] = deliv[it, rows, cols] + ring[it, 0, :, cols]
+        rows = part(before, HR, HR)
+        deliv[it, rows, cols] = deliv[it, rows, cols] + ring[it, 1, :, cols]
+        go(it, i, deliv.at[it, part(after, 0, QR), cols], from_x.at[it, 0, :, cols], rs2_r, right)
+        go(it, i, deliv.at[it, part(before, 0, QR), cols], from_x.at[it, 1, :, cols], rs2_r, left)
 
     def ag1(it, i):
         cols = half(i, core)
@@ -304,18 +280,19 @@
             go(it, i, piece, piece, ag1_r, xs[1])
 
     def ag2(it, i):
-        wait_for(two(from_x, QR, 2 if AG_RING[it][i] else 3), ag1_r.at[i])
-        if AG_RING[it][i]:
-            cols = half(i, core)
-            out = r1 if it == 0 else r_ref
-            piece = out.at[part(before, 0, HR), cols]
-            go(it, i, piece, piece, ag2_r, right)
-            piece = out.at[part(after, HR, HR), cols]
-            go(it, i, piece, piece, ag2_r, left)
+        wait_for(two(from_x, QR), ag1_r.at[i])
+        cols = half(i, core)
+        out = r1 if it == 0 else r_ref
+        piece = out.at[part(before, 0, HR), cols]
+        go(it, i, piece, piece, ag2_r, right)
+        piece = out.at[part(after, HR, HR), cols]
+        go(it, i, piece, piece, ag2_r, left)
 
     def sibb(it, i):
         if AG_RING[it][i]:
             wait_for(two(ring, HR), ag2_r.at[i])
+        else:
+            wait_for(two(from_x, QR, 3), ag1_r.at[i])
         out = r1 if it == 0 else r_ref
         piece = out.at[:, half(i, core)]
         go(it, i, piece, piece, sibb_r, sib)

time: 57.3 us -> 53 us (0.925)
  Pallas kernels: 56.5 us -> 52.3 us
    pallas_call x1, Pallas kernels: 53.2 us -> 49 us  [shards(): pl.pallas_call(kernel, out_shape=outs, in_specs=[anywhere] * 13, out_spec...]
where the time goes in v4:
time: 53 us; the launch traced here: 52.9 us
  Pallas kernels  52.3 us (99%)
  between operations  0.64 us (1%)
    pallas_call x1, Pallas kernels, shards(): pl.pallas_call(kernel, out_shape=outs, in_specs=[anywhere] * 13, out_spec...  49 us
    pallas_call x1, Pallas kernels, shards(): pl.pallas_call(write_out, out_shape=tuple((pltpu.HBM(o.shape, o.dtype) fo...  3.29 us

profile of v4, /device:TPU:1, one launch (start us, length us, event | category | flops | bytes accessed | tf_op | source)
XLA Modules:
  0.0 52.9 jit_solution(10382084220279552714)
XLA Ops:
  0.6 49.0 %shard_map.156 = (f32[4,192,2048]{2,1,0:T(8,128)S(1)}, f32[4,192]{1,0:T(4,128)S(1)}, f32[192,2048]{1,0:T(8,128)S(1)}, f32[4,2048]{1,0:T(4,128)S(1)}) custom-call(f32[4,192,2048]{2,1,0:T(8,128)} %x0_hbm.1, f32[4,192]{1,0:T(4,128)} %s0_hbm.1, f32[192,2048]{1,0:T(8,128)} %r0_hbm.1, f32[4,2048]{1,0:T(4,128)} %p0_hbm.1, f32[192,2048]{1,0:T(8,128)} %value_hbm.1, ...), custom_call_target="tpu_custom_call" | custom-call | tf_op jit(solution)/shard_map/pallas_call | solution.py:485
  49.6 3.3 %shard_map.157 = (f32[4,192,2048]{2,1,0:T(8,128)}, f32[4,192]{1,0:T(4,128)}, f32[192,2048]{1,0:T(8,128)}, f32[4,2048]{1,0:T(4,128)}) custom-call(f32[4,192,2048]{2,1,0:T(8,128)S(1)} %get-tuple-element.8.x, f32[4,192]{1,0:T(4,128)S(1)} %get-tuple-element.9.s, f32[192,2048]{1,0:T(8,128)S(1)} %get-tuple-element.10.r, f32[4,2048]{1,0:T(4,128)S(1)} %get-tuple-element.11.p), custom_call_target="tpu_custom_call" | custom-call | tf_op jit(solution)/shard_map/pallas_call | solution.py:496

commit v5 on v4

v5 whole, which is shorter than its diff:
```python
import jax
import jax.numpy as jnp
from jax import lax
from jax.experimental import pallas as pl
from jax.experimental.pallas import tpu as pltpu
from jax.sharding import PartitionSpec as P

S = 192
SEG_BLOCK = 8
SLOTS = 32
CAMPAIGNS = 32768
MESH = pl.DeviceIdType.MESH
HIGHEST = lax.Precision.HIGHEST

NT = 4
NU = 2 * NT
CD = 2048
CW = CD // 2
NC = CW // 128
QR = S // 4
HR = QR // 2
NG = 2
GC = NC // NG
BLOCKED = -1e30

SIG_SUPPLY = 4.0 / CAMPAIGNS
SIG_REACH = 1.0 / (2 * SLOTS)
SIG_SPEND = 1.0 / (S * SLOTS * SLOTS)

RS_RING = ((0, 0, 0, 1, 1, 1, 1, 0), (1, 0, 1, 0, 1, 0, 0, 1))
AG_RING = ((1, 0, 0, 0, 0, 0, 0, 1), (0, 1, 1, 1, 0, 1, 1, 0))
ORDER = (
    ("comp", 0, 0), ("rs1", 0, 0), ("comp", 0, 6), ("comp", 0, 7), ("rs1", 0, 6), ("rs1", 0, 7), ("caps",),
    ("comp", 0, 5), ("comp", 0, 3), ("rs1", 0, 3), ("comp", 0, 4), ("sp1", 0, 1), ("rs1", 0, 4),
    ("rs1", 0, 5), ("comp", 0, 2), ("rs1", 0, 2), ("comp", 0, 1), ("uz", 0), ("rs1", 0, 1), ("rs2", 0, 6),
    ("ag1", 0, 0), ("sp1", 0, 0), ("ag1", 0, 7), ("rs2", 0, 5), ("uy", 0), ("rs2", 0, 4), ("ag1", 0, 2),
    ("rs2", 0, 3), ("sp2", 0, 1), ("ag1", 0, 6), ("ag2", 0, 0), ("sp2", 0, 0), ("ag2", 0, 7), ("ag1", 0, 1),
    ("us", 0), ("ag1", 0, 4), ("fin", 0, 2), ("ag1", 0, 5), ("ag1", 0, 3), ("ue", 0), ("fin", 0, 6),
    ("sp3", 1), ("comp", 1, 6), ("rs1", 1, 6), ("sp3", 0), ("fin", 0, 7), ("fin", 0, 0), ("comp", 1, 2),
    ("comp", 1, 7), ("rs1", 1, 7), ("fin", 0, 1), ("comp", 1, 1), ("rs1", 1, 2), ("rs1", 1, 1), ("fin", 0, 4),
    ("comp", 1, 4), ("rs1", 1, 4), ("comp", 1, 0), ("rs1", 1, 0), ("fin", 0, 5), ("comp", 1, 5),
    ("rs1", 1, 5), ("fin", 0, 3), ("comp", 1, 3), ("rs1", 1, 3), ("xo", 0, 8), ("ag1", 1, 6), ("rs2", 1, 2),
    ("rs2", 1, 4), ("rs2", 1, 7), ("ag1", 1, 1), ("rs2", 1, 0), ("ag1", 1, 5), ("uz", 1), ("ag1", 1, 3),
    ("ag2", 1, 6), ("ag1", 1, 2), ("ag1", 1, 4), ("ag2", 1, 1), ("ag1", 1, 7), ("uy", 1), ("ag1", 1, 0),
    ("ag2", 1, 5), ("ag2", 1, 3), ("sibb", 1, 6), ("ag2", 1, 2), ("sp1", 1, 0), ("sp1", 1, 1), ("fin", 1, 6),
    ("sibb", 1, 1), ("sibb", 1, 4), ("sibb", 1, 7), ("fin", 1, 1), ("us", 1), ("fin", 1, 4), ("sibb", 1, 0),
    ("sibb", 1, 5), ("sibb", 1, 3), ("sibb", 1, 2), ("fin", 1, 7), ("fin", 1, 0), ("sp2", 1, 0),
    ("fin", 1, 5), ("ue", 1), ("sp2", 1, 1), ("pf1",), ("fin", 1, 3), ("fin", 1, 2), ("pf2",),
)


FIRST = [where[1] for name, *where in ORDER if name == "comp" and where[0] == 0]


def kernel(
    x0_hbm, s0_hbm, r0_hbm, p0_hbm, value_hbm, share_hbm, price_hbm, rcap_hbm,
    limit_hbm, supply_hbm, elig_hbm, begin_hbm, span_hbm,
    x_out, s_out, r_out, p_out,
    p0_ref, limit_ref, elig_ref, begin_ref, span_ref, rows_ref,
    x0, x1, value, share, price, r0, rcap,
    deliv, ring, from_x, r1,
    pen, sb, s8, s1, used, uz, uy, us,
    pka, pk0, pk1, pres, pin, cap, live, zeff, spent, tsum, tstart, tots,
    ld, x_s, x_r, xo, start_s, start_r, sent, rs1_r, rs2_r, ag1_r, ag2_r, sibb_r,
    tot_s, tot_r, used_s, used_r, pf,
):
    camp = lax.axis_index("camp")
    tm = lax.axis_index("tm")
    y, z = camp // 4, camp % 4
    x, core = tm // 2, tm % 2
    other = 1 - core
    sib = (camp, x * 2 + other)
    xs = [(camp, ((x + d) % 4) * 2 + core) for d in (1, 2, 3)]
    tms = [(camp, (tm + d) % 8) for d in range(1, 8)]
    zs = [(y * 4 + (z + d) % 4, tm) for d in (1, 2, 3)]
    ys = [(((y + d) % 4) * 4 + z, tm) for d in (1, 2, 3)]
    right, left = xs[0], xs[2]
    my_slots, sib_slots = pl.ds(core * NT, NT), pl.ds(other * NT, NT)
    my_tiles = pl.ds(pl.multiple_of(core * NC, 8), NC)
    sib_tiles = pl.ds(pl.multiple_of(other * NC, 8), NC)

    def lanes(of_core, first, width):
        return pl.ds(pl.multiple_of(of_core * CW + first, 128), width)

    my_lanes = lanes(core, 0, CW)

    def wait_for(like, sem):
        pltpu.make_async_copy(like, like, sem).wait()

    def send(src, dst, ssem, rsem, to):
        return pltpu.make_async_remote_copy(
            src_ref=src, dst_ref=dst, send_sem=ssem, recv_sem=rsem, device_id=to, device_id_type=MESH
        )

    barrier = pltpu.get_barrier_semaphore()
    greet = tms + zs + ys
    for to in greet:
        pl.semaphore_signal(barrier, inc=1, device_id=to, device_id_type=MESH)

    loads = []

    def load(src, dst):
        cp = pltpu.make_async_copy(src, dst, ld.at[len(loads)])
        cp.start()
        loads.append(cp)

    load(p0_hbm, p0_ref)
    load(s0_hbm, rows_ref.at[core, 0])
    load(supply_hbm, rows_ref.at[core, 1])
    for src, dst in (
        (begin_hbm, begin_ref), (span_hbm, span_ref), (limit_hbm, limit_ref),
    ):
        load(src, dst)
    load(elig_hbm.at[:, my_lanes], elig_ref)
    small = len(loads)
    load(value_hbm.at[:, my_lanes], value)
    load(x0_hbm.at[:, :, my_lanes], x0.at[my_slots])
    load(share_hbm.at[:, my_lanes], share)
    load(price_hbm.at[:, my_lanes], price)
    load(r0_hbm.at[:, my_lanes], r0)
    load(rcap_hbm.at[pl.ds(pl.multiple_of(x * QR, 8), QR), my_lanes], rcap)

    for cp in loads[:small]:
        cp.wait()
    for t in range(NT):
        for k in range(2 * NC):
            pka[t, k : k + 1, :] = p0_ref[t : t + 1, k * 128 : (k + 1) * 128]
    tstart[pl.ds(2 * x, 2)] = jnp.zeros((2, NC, 128), jnp.float32)
    tsum[...] = pka[0] + pka[1] + pka[2] + pka[3]
    for t in range(NT):
        pk0[core * NT + t] = pka[t, my_tiles, :]

    begin = begin_ref[my_tiles, :]
    span = span_ref[my_tiles, :]
    limit = limit_ref[my_tiles, :]
    for u in range(NU):
        slot = x * NU + u
        live[u] = ((slot >= begin) & (slot < begin + span)).astype(jnp.float32)

    pl.semaphore_wait(barrier, len(greet))

    for d in (1, 2, 3):
        for c in (0, 1):
            to = (camp, ((x + d) % 4) * 2 + c)
            send(tsum.at[pl.ds(c * NC, NC)], tstart.at[tm], start_s.at[0], start_r.at[0], to).start()
    send(pka.at[:, sib_tiles], pk0.at[my_slots], start_s.at[1], start_r.at[1], sib).start()
    send(rows_ref.at[core], rows_ref.at[core], start_s.at[2], start_r.at[2], sib).start()
    for q in FIRST:
        send(
            x0_hbm.at[:, :, lanes(other, q * 128, 128)], x0.at[my_slots, :, pl.ds(q * 128, 128)], x_s.at[0], x_r.at[q], sib
        ).start()

    def spread_supply(rows):
        s8[...] = rows * -0.5
        table = s8[...]
        for u in range(NU):
            pick = (lax.broadcasted_iota(jnp.int32, (8, 128), 0) == u).astype(jnp.float32)
            sb[u] = lax.dot_general(
                table, pick, (((0,), (0,)), ((), ())), precision=HIGHEST, preferred_element_type=jnp.float32
            )

    for b in range(S // SEG_BLOCK):
        pen[b] = jnp.where(elig_ref[b : b + 1, :] > 0, 0.0, BLOCKED)
    loads[small].wait()

    def value_body(rb, carry):
        rows = pl.ds(pl.multiple_of(rb * 8, 8), 8)
        value[rows, :] = 0.5 * value[rows, :] + pen[rb]
        return carry

    lax.fori_loop(0, S // 8, value_body, 0)
    used[...] = jnp.zeros_like(used)
    for sem in (start_s, start_r):
        wait_for(rows_ref.at[0], sem.at[2])
    s0 = jnp.concatenate([rows_ref[0, 0], rows_ref[1, 0]], axis=0)
    s1[...] = s0
    spread_supply(s0)
    for cp in loads[small + 1 :]:
        cp.wait()

    def masked_total(parts, senders, mine, later):
        total = None
        for m in range(senders):
            keep = (m > mine) if later else (m < mine)
            term = jnp.where(keep, parts(m), 0.0)
            total = term if total is None else total + term
        return total

    def set_zeff(duals, later, rows):
        run = later
        for u in reversed(range(NU)):
            run = run + duals[u]
            zeff[u, rows, :] = jnp.where(live[u, rows, :] > 0.0, -0.5 * run, BLOCKED)

    for sem in (start_s, start_r):
        wait_for(tstart.at[pl.ds(0, 6)], sem.at[0])
        wait_for(pk0.at[pl.ds(0, NT)], sem.at[1])
    set_zeff(
        [pk0[u] for u in range(NU)],
        masked_total(lambda m: tstart[2 * m] + tstart[2 * m + 1], 4, x, True),
        slice(0, NC),
    )

    def comp(it, i):
        cols = pl.ds(i * 128, 128)
        zb = [jnp.broadcast_to(zeff[u, i : i + 1, :], (8, 128)) for u in range(NU)]

        def body(rb, acc):
            rows = pl.ds(pl.multiple_of(rb * 8, 8), 8)
            acc = list(acc)
            sh = share[rows, cols]
            pr = price[rows, cols]
            rd = r0[rows, cols] if it == 0 else r1[rows, cols]
            base = value[rows, cols] - 0.5 * rd
            total = None
            for u in range(NU):
                old = x0[u, rows, cols] if it == 0 else x1[u, rows, cols]
                new = jnp.maximum((old + base) + (sh * sb[u, rows, :] + pr * zb[u]), 0.0)
                bar = (new + new) - old
                acc[u] = acc[u] + pr * bar
                used[u, rows, :] = used[u, rows, :] + sh * bar
                total = bar if total is None else total + bar
                if it == 0:
                    x1[u, rows, cols] = new
                else:
                    x1[u, rows, cols] = (2.0 / 3.0) * bar + (1.0 / 3.0) * x0[u, rows, cols]
            deliv[it, rows, cols] = total
            return tuple(acc)

        zero = jnp.zeros((8, 128), jnp.float32)
        acc = lax.fori_loop(0, S // 8, body, (zero,) * NU, unroll=2)
        for u in range(NU):
            spent[it, u, i : i + 1, :] = jnp.sum(acc[u], axis=0, keepdims=True)

    def part(chip, first, rows):
        return pl.ds(pl.multiple_of(chip * QR + first, 8), rows)

    opposite, after, before = (x + 2) % 4, (x + 1) % 4, (x + 3) % 4

    def two(buf, rows, n=2):
        return buf.at[0, pl.ds(0, n), pl.ds(0, rows), pl.ds(0, 128)]

    def go(it, i, src, dst, rsem, to):
        send(src, dst, sent.at[it], rsem.at[i], to).start()

    def held(it, i):
        if it == 0:
            return r1, pl.ds(i * 128, 128)
        return r_out, lanes(core, i * 128, 128)

    def chunk(it, i):
        if it == 0:
            wait_for(x0.at[pl.ds(0, NT), :, pl.ds(0, 128)], x_r.at[i])
        comp(it, i)

    def hand_over(i, n):
        cols = pl.ds(i * 128, n * 128)
        to = x_out.at[:, :, lanes(core, i * 128, n * 128)]
        send(x1.at[sib_slots, :, cols], to, xo.at[0], xo.at[1], sib).start()
        pltpu.make_async_copy(x1.at[my_slots, :, cols], to, xo.at[2]).start()

    def rs1(it, i):
        cols = pl.ds(i * 128, 128)
        if RS_RING[it][i]:
            go(it, i, deliv.at[it, part(opposite, 0, HR), cols], ring.at[it, 0, :, cols], rs1_r, right)
            go(it, i, deliv.at[it, part(opposite, HR, HR), cols], ring.at[it, 1, :, cols], rs1_r, left)
        else:
            for d, chip, to in ((0, after, xs[0]), (1, before, xs[2]), (2, opposite, xs[1])):
                go(it, i, deliv.at[it, part(chip, 0, QR), cols], from_x.at[it, d, :, cols], rs2_r, to)

    def rs2(it, i):
        cols = pl.ds(i * 128, 128)
        wait_for(two(ring, HR), rs1_r.at[i])
        rows = part(after, 0, HR)
        deliv[it, rows, cols] = deliv[it, rows, cols] + ring[it, 0, :, cols]
        rows = part(before, HR, HR)
        deliv[it, rows, cols] = deliv[it, rows, cols] + ring[it, 1, :, cols]
        go(it, i, deliv.at[it, part(after, 0, QR), cols], from_x.at[it, 0, :, cols], rs2_r, right)
        go(it, i, deliv.at[it, part(before, 0, QR), cols], from_x.at[it, 1, :, cols], rs2_r, left)

    def ag1(it, i):
        cols = pl.ds(i * 128, 128)
        rows = part(x, 0, QR)
        wait_for(two(from_x, QR, 2 if RS_RING[it][i] else 3), rs2_r.at[i])
        total = deliv[it, rows, cols] + from_x[it, 0, :, cols] + from_x[it, 1, :, cols]
        if not RS_RING[it][i]:
            total = total + from_x[it, 2, :, cols]
        start = r0[rows, cols]
        out, where = held(it, i)
        if it == 0:
            r1[rows, cols] = jnp.maximum(start + SIG_REACH * (total - rcap[:, cols]), 0.0)
        else:
            old = r1[rows, cols]
            new = jnp.maximum(old + SIG_REACH * (total - rcap[:, cols]), 0.0)
            r_out[rows, where] = (2.0 / 3.0) * (2.0 * new - old) + (1.0 / 3.0) * start
        piece = out.at[rows, where]
        go(it, i, piece, piece, ag1_r, right)
        go(it, i, piece, piece, ag1_r, left)
        if not AG_RING[it][i]:
            go(it, i, piece, piece, ag1_r, xs[1])

    def ag2(it, i):
        wait_for(two(from_x, QR), ag1_r.at[i])
        out, where = held(it, i)
        piece = out.at[part(before, 0, HR), where]
        go(it, i, piece, piece, ag2_r, right)
        piece = out.at[part(after, HR, HR), where]
        go(it, i, piece, piece, ag2_r, left)

    def gathered(it, i):
        if AG_RING[it][i]:
            wait_for(two(ring, HR), ag2_r.at[i])
        else:
            wait_for(two(from_x, QR, 3), ag1_r.at[i])

    def sibb(it, i):
        gathered(it, i)
        piece = r_out.at[:, lanes(core, i * 128, 128)]
        go(it, i, piece, piece, sibb_r, sib)

    def fin(it, i):
        if it == 0:
            gathered(it, i)
        else:
            wait_for(deliv.at[0, :, pl.ds(0, 128)], sibb_r.at[i])

    def used_z(it):
        total = None
        for u in range(NU):
            term = lax.dot_general(
                jnp.ones((8, 128), jnp.float32), used[u], (((1,), (1,)), ((), ())),
                precision=HIGHEST, preferred_element_type=jnp.float32,
            )
            term = jnp.where(lax.broadcasted_iota(jnp.int32, (8, S), 0) == u, term, 0.0)
            total = term if total is None else total + term
        uz[it, z] = total
        for to in zs:
            send(uz.at[it, z], uz.at[it, z], used_s.at[it, 0], used_r.at[it, 0], to).start()
        if it == 0:
            used[...] = jnp.zeros_like(used)

    def used_y(it):
        for sem in (used_s, used_r):
            wait_for(uz.at[it, pl.ds(0, 3)], sem.at[it, 0])
        uy[it, y] = uz[it, 0] + uz[it, 1] + uz[it, 2] + uz[it, 3]
        for to in ys:
            send(uy.at[it, y], uy.at[it, y], used_s.at[it, 1], used_r.at[it, 1], to).start()

    def used_sib(it):
        for sem in (used_s, used_r):
            wait_for(uy.at[it, pl.ds(0, 3)], sem.at[it, 1])
        us[it, core] = uy[it, 0] + uy[it, 1] + uy[it, 2] + uy[it, 3]
        send(us.at[it, core], us.at[it, core], used_s.at[it, 2], used_r.at[it, 2], sib).start()

    def used_end(it):
        for sem in (used_s, used_r):
            wait_for(us.at[it, 0], sem.at[it, 2])
        total = us[it, 0] + us[it, 1]
        supply = jnp.concatenate([rows_ref[0, 1], rows_ref[1, 1]], axis=0)
        old = s1[...]
        new = jnp.maximum(old + SIG_SUPPLY * (total - supply), 0.0)
        if it == 0:
            s1[...] = new
            spread_supply(new)
        else:
            first = jnp.concatenate([rows_ref[0, 0], rows_ref[1, 0]], axis=0)
            res = (2.0 / 3.0) * (2.0 * new - old) + (1.0 / 3.0) * first
            s_out[...] = jnp.where(core == 0, res[0:NT], res[NT:NU])

    def share_total(e, g, total):
        tots[e, g, x] = total
        for to in xs:
            send(tots.at[e, g, x], tots.at[e, g, x], tot_s.at[e, g], tot_r.at[e, g], to).start()

    def wait_total(e, g, later):
        for sem in (tot_s, tot_r):
            wait_for(tots.at[e, g, pl.ds(0, 3)], sem.at[e, g])
        return masked_total(lambda m: tots[e, g, m], 4, x, later)

    def add_up(terms):
        total = terms[0]
        for term in terms[1:]:
            total = total + term
        return total

    def spend_1(it, g):
        rows = slice(g * GC, (g + 1) * GC)
        share_total(2 * it, g, add_up([spent[it, u, rows] for u in range(NU)]))

    def spend_2(it, g):
        rows = slice(g * GC, (g + 1) * GC)
        run = wait_total(2 * it, g, False)
        fresh = []
        for u in range(NU):
            run = run + spent[it, u, rows]
            old = pk0[u, rows] if it == 0 else pk1[u, rows]
            new = jnp.maximum(old + SIG_SPEND * (run - cap[u, rows]), 0.0)
            if it == 0:
                pk1[u, rows] = new
                fresh.append(new)
            else:
                pres[u, rows] = (2.0 / 3.0) * (2.0 * new - old) + (1.0 / 3.0) * pk0[u, rows]
        if it == 0:
            share_total(1, g, add_up(fresh))

    def spend_3(g):
        rows = slice(g * GC, (g + 1) * GC)
        later = wait_total(1, g, True)
        set_zeff([pk1[u, rows] for u in range(NU)], later, rows)

    def spend_out():
        send(pres.at[sib_slots], pin, pf.at[0], pf.at[1], sib).start()

    def spend_end():
        wait_for(pin, pf.at[0])
        wait_for(pin, pf.at[1])
        for t in range(NT):
            for k in range(NC):
                p_out[t : t + 1, lanes(core, k * 128, 128)] = pres[core * NT + t, k : k + 1, :]
                p_out[t : t + 1, lanes(other, k * 128, 128)] = pin[t, k : k + 1, :]

    def caps():
        for u in range(NU):
            frac = jnp.clip((x * NU + u + 1 - begin).astype(jnp.float32) / span.astype(jnp.float32), 0.0, 1.0)
            cap[u] = limit * frac

    steps = dict(
        comp=chunk, rs1=rs1, rs2=rs2, ag1=ag1, ag2=ag2, sibb=sibb, fin=fin, uz=used_z, uy=used_y, us=used_sib,
        ue=used_end, sp1=spend_1, sp2=spend_2, sp3=spend_3, caps=caps, pf1=spend_out, pf2=spend_end, xo=hand_over,
    )
    for name, *where in ORDER:
        steps[name](*where)
    wait_for(x0.at[pl.ds(0, NT)], x_s.at[0])
    for k in range(3):
        wait_for(x0.at[pl.ds(0, NT)], xo.at[k])
    wait_for(x0.at[pl.ds(0, 3), pl.ds(0, S // 2)], sent.at[0])
    wait_for(x0.at[pl.ds(0, 5), pl.ds(0, S // 2)], sent.at[1])


def write_out(x, s, r, p, x_hbm, s_hbm, r_hbm, p_hbm, sem):
    cps = []

    def store(src, dst):
        cp = pltpu.make_async_copy(src, dst, sem.at[len(cps)])
        cp.start()
        cps.append(cp)

    store(s, s_hbm)
    store(p, p_hbm)
    for t in range(NT):
        store(x.at[t], x_hbm.at[t])
    store(r, r_hbm)
    for cp in cps:
        cp.wait()


def shards(
    primal_start, supply_start, reach_start, spend_start, value, share, price, reach_cap,
    spend_limit, supply, eligible, start_slot, active_span,
):
    f32 = jnp.float32
    vmem = pl.BlockSpec(memory_space=pltpu.VMEM)
    anywhere = pl.BlockSpec(memory_space=pltpu.HBM)
    dma = pltpu.SemaphoreType.DMA
    outs = (
        pltpu.VMEM((NT, S, CD), f32),
        pltpu.VMEM((NT, S), f32),
        pltpu.VMEM((S, CD), f32),
        pltpu.VMEM((NT, CD), f32),
    )
    scratch = [
        pltpu.VMEM((NT, CD), f32),
        pltpu.VMEM((2 * NC, 128), f32),
        pltpu.VMEM((S // SEG_BLOCK, CW), jnp.int32),
        pltpu.VMEM((2 * NC, 128), jnp.int32),
        pltpu.VMEM((2 * NC, 128), jnp.int32),
        pltpu.VMEM((2, 2, NT, S), f32),
        pltpu.VMEM((NU, S, CW), f32),
        pltpu.VMEM((NU, S, CW), f32),
        pltpu.VMEM((S, CW), f32),
        pltpu.VMEM((S, CW), f32),
        pltpu.VMEM((S, CW), f32),
        pltpu.VMEM((S, CW), f32),
        pltpu.VMEM((QR, CW), f32),
        pltpu.VMEM((2, S, CW), f32),
        pltpu.VMEM((2, 2, HR, CW), f32),
        pltpu.VMEM((2, 3, QR, CW), f32),
        pltpu.VMEM((S, CW), f32),
        pltpu.VMEM((S // SEG_BLOCK, 1, CW), f32),
        pltpu.VMEM((NU, S, 128), f32),
        pltpu.VMEM((NU, S), f32),
        pltpu.VMEM((NU, S), f32),
        pltpu.VMEM((NU, S, 128), f32),
        pltpu.VMEM((2, 4, NU, S), f32),
        pltpu.VMEM((2, 4, NU, S), f32),
        pltpu.VMEM((2, 2, NU, S), f32),
        pltpu.VMEM((NT, 2 * NC, 128), f32),
        pltpu.VMEM((NU, NC, 128), f32),
        pltpu.VMEM((NU, NC, 128), f32),
        pltpu.VMEM((NU, NC, 128), f32),
        pltpu.VMEM((NT, NC, 128), f32),
        pltpu.VMEM((NU, NC, 128), f32),
        pltpu.VMEM((NU, NC, 128), f32),
        pltpu.VMEM((NU, NC, 128), f32),
        pltpu.VMEM((2, NU, NC, 128), f32),
        pltpu.VMEM((2 * NC, 128), f32),
        pltpu.VMEM((8, NC, 128), f32),
        pltpu.VMEM((3, NG, 4, GC, 128), f32),
        dma((13,)),
        dma((1,)), dma((NC,)), dma((3,)),
        dma((3,)), dma((3,)),
        dma((2,)),
        dma((NC,)), dma((NC,)), dma((NC,)), dma((NC,)), dma((NC,)),
        dma((3, NG)), dma((3, NG)),
        dma((2, 3)), dma((2, 3)),
        dma((2,)),
    ]
    args = (
        primal_start, supply_start, reach_start, spend_start, value, share, price, reach_cap,
        spend_limit.reshape(2 * NC, 128), supply, eligible,
        start_slot.reshape(2 * NC, 128), active_span.reshape(2 * NC, 128),
    )
    res = pl.pallas_call(
        kernel,
        out_shape=outs,
        in_specs=[anywhere] * 13,
        out_specs=(vmem,) * 4,
        scratch_shapes=scratch,
        compiler_params=pltpu.CompilerParams(
            collective_id=0, has_side_effects=True, vmem_limit_bytes=44 * 2**20
        ),
    )(*[pltpu.with_memory_space_constraint(a, pltpu.HBM) for a in args])
    return tuple(
        pl.pallas_call(
            write_out,
            out_shape=tuple(pltpu.HBM(o.shape, o.dtype) for o in outs),
            in_specs=[vmem] * 4,
            out_specs=(anywhere,) * 4,
            scratch_shapes=[dma((NT + 3,))],
            compiler_params=pltpu.CompilerParams(vmem_limit_bytes=2**20),
        )(*res)
    )


def solution(mesh):
    in_specs = (
        P("tm", None, "camp"), P("tm", None), P(None, "camp"), P("tm", "camp"),
        P(None, "camp"), P(None, "camp"), P(None, "camp"), P(None, "camp"),
        P("camp"), P("tm", None), P(None, "camp"), P("camp"), P("camp"),
    )
    out_specs = (P("tm", None, "camp"), P("tm", None), P(None, "camp"), P("tm", "camp"))
    return jax.shard_map(shards, mesh=mesh, in_specs=in_specs, out_specs=out_specs, check_vma=False)
```

time: 53 us -> 51.4 us (0.970)
  Pallas kernels: 52.3 us -> 50.6 us
    pallas_call x1, Pallas kernels: 49 us -> 47.4 us  [shards(): pl.pallas_call(kernel, out_shape=outs, in_specs=[anywhere] * 13, out_spec...]
where the time goes in v5:
time: 51.4 us; the launch traced here: 51.2 us
  Pallas kernels  50.6 us (98%)
  between operations  0.64 us (1%)
    pallas_call x1, Pallas kernels, shards(): pl.pallas_call(kernel, out_shape=outs, in_specs=[anywhere] * 13, out_spec...  47.4 us
    pallas_call x1, Pallas kernels, shards(): pl.pallas_call(write_out, out_shape=tuple((pltpu.HBM(o.shape, o.dtype) fo...  3.25 us

profile of v5, /device:TPU:1, one launch (start us, length us, event | category | flops | bytes accessed | tf_op | source)
XLA Modules:
  0.0 51.2 jit_solution(13425756129040771982)
XLA Ops:
  0.6 47.4 %shard_map.156 = (f32[4,192,2048]{2,1,0:T(8,128)S(1)}, f32[4,192]{1,0:T(4,128)S(1)}, f32[192,2048]{1,0:T(8,128)S(1)}, f32[4,2048]{1,0:T(4,128)S(1)}) custom-call(f32[4,192,2048]{2,1,0:T(8,128)} %x0_hbm.1, f32[4,192]{1,0:T(4,128)} %s0_hbm.1, f32[192,2048]{1,0:T(8,128)} %r0_hbm.1, f32[4,2048]{1,0:T(4,128)} %p0_hbm.1, f32[192,2048]{1,0:T(8,128)} %value_hbm.1, ...), custom_call_target="tpu_custom_call" | custom-call | tf_op jit(solution)/shard_map/pallas_call | solution.py:523
  48.0 3.2 %shard_map.157 = (f32[4,192,2048]{2,1,0:T(8,128)}, f32[4,192]{1,0:T(4,128)}, f32[192,2048]{1,0:T(8,128)}, f32[4,2048]{1,0:T(4,128)}) custom-call(f32[4,192,2048]{2,1,0:T(8,128)S(1)} %get-tuple-element.8.x, f32[4,192]{1,0:T(4,128)S(1)} %get-tuple-element.9.s, f32[192,2048]{1,0:T(8,128)S(1)} %get-tuple-element.10.r, f32[4,2048]{1,0:T(4,128)S(1)} %get-tuple-element.11.p), custom_call_target="tpu_custom_call" | custom-call | tf_op jit(solution)/shard_map/pallas_call | solution.py:534

commit v6 on v5

--- a/solution.py
+++ b/solution.py
@@ -40,12 +40,12 @@
     ("comp", 1, 7), ("rs1", 1, 7), ("fin", 0, 1), ("comp", 1, 1), ("rs1", 1, 2), ("rs1", 1, 1), ("fin", 0, 4),
     ("comp", 1, 4), ("rs1", 1, 4), ("comp", 1, 0), ("rs1", 1, 0), ("fin", 0, 5), ("comp", 1, 5),
     ("rs1", 1, 5), ("fin", 0, 3), ("comp", 1, 3), ("rs1", 1, 3), ("xo", 0, 8), ("ag1", 1, 6), ("rs2", 1, 2),
-    ("rs2", 1, 4), ("rs2", 1, 7), ("ag1", 1, 1), ("rs2", 1, 0), ("ag1", 1, 5), ("uz", 1), ("ag1", 1, 3),
+    ("rs2", 1, 4), ("rs2", 1, 7), ("ag1", 1, 1), ("rs2", 1, 0), ("ag1", 1, 5), ("uz", 1), ("sp1", 1, 0), ("sp1", 1, 1), ("ag1", 1, 3),
     ("ag2", 1, 6), ("ag1", 1, 2), ("ag1", 1, 4), ("ag2", 1, 1), ("ag1", 1, 7), ("uy", 1), ("ag1", 1, 0),
-    ("ag2", 1, 5), ("ag2", 1, 3), ("sibb", 1, 6), ("ag2", 1, 2), ("sp1", 1, 0), ("sp1", 1, 1), ("fin", 1, 6),
+    ("ag2", 1, 5), ("ag2", 1, 3), ("sibb", 1, 6), ("ag2", 1, 2), ("sp2", 1, 0), ("sp2", 1, 1), ("pf1",), ("fin", 1, 6),
     ("sibb", 1, 1), ("sibb", 1, 4), ("sibb", 1, 7), ("fin", 1, 1), ("us", 1), ("fin", 1, 4), ("sibb", 1, 0),
-    ("sibb", 1, 5), ("sibb", 1, 3), ("sibb", 1, 2), ("fin", 1, 7), ("fin", 1, 0), ("sp2", 1, 0),
-    ("fin", 1, 5), ("ue", 1), ("sp2", 1, 1), ("pf1",), ("fin", 1, 3), ("fin", 1, 2), ("pf2",),
+    ("sibb", 1, 5), ("sibb", 1, 3), ("sibb", 1, 2), ("fin", 1, 7), ("fin", 1, 0),
+    ("fin", 1, 5), ("ue", 1),  ("pf2",), ("fin", 1, 3), ("fin", 1, 2),
 )
 
 
@@ -228,7 +228,7 @@
             return tuple(acc)
 
         zero = jnp.zeros((8, 128), jnp.float32)
-        acc = lax.fori_loop(0, S // 8, body, (zero,) * NU, unroll=2)
+        acc = lax.fori_loop(0, S // 8, body, (zero,) * NU, unroll=4)
         for u in range(NU):
             spent[it, u, i : i + 1, :] = jnp.sum(acc[u], axis=0, keepdims=True)
 

time: 51.4 us -> 51.3 us (level)
  no operation moved by 1% of the time
where the time goes in v6:
time: 51.3 us; the launch traced here: 51.2 us
  Pallas kernels  50.5 us (98%)
  between operations  0.64 us (1%)
    pallas_call x1, Pallas kernels, shards(): pl.pallas_call(kernel, out_shape=outs, in_specs=[anywhere] * 13, out_spec...  47.3 us
    pallas_call x1, Pallas kernels, shards(): pl.pallas_call(write_out, out_shape=tuple((pltpu.HBM(o.shape, o.dtype) fo...  3.25 us

profile of v6, /device:TPU:1, one launch (start us, length us, event | category | flops | bytes accessed | tf_op | source)
XLA Modules:
  0.0 51.2 jit_solution(10846795573950822301)
XLA Ops:
  0.6 47.3 %shard_map.156 = (f32[4,192,2048]{2,1,0:T(8,128)S(1)}, f32[4,192]{1,0:T(4,128)S(1)}, f32[192,2048]{1,0:T(8,128)S(1)}, f32[4,2048]{1,0:T(4,128)S(1)}) custom-call(f32[4,192,2048]{2,1,0:T(8,128)} %x0_hbm.1, f32[4,192]{1,0:T(4,128)} %s0_hbm.1, f32[192,2048]{1,0:T(8,128)} %r0_hbm.1, f32[4,2048]{1,0:T(4,128)} %p0_hbm.1, f32[192,2048]{1,0:T(8,128)} %value_hbm.1, ...), custom_call_target="tpu_custom_call" | custom-call | tf_op jit(solution)/shard_map/pallas_call | solution.py:523
  47.9 3.2 %shard_map.157 = (f32[4,192,2048]{2,1,0:T(8,128)}, f32[4,192]{1,0:T(4,128)}, f32[192,2048]{1,0:T(8,128)}, f32[4,2048]{1,0:T(4,128)}) custom-call(f32[4,192,2048]{2,1,0:T(8,128)S(1)} %get-tuple-element.8.x, f32[4,192]{1,0:T(4,128)S(1)} %get-tuple-element.9.s, f32[192,2048]{1,0:T(8,128)S(1)} %get-tuple-element.10.r, f32[4,2048]{1,0:T(4,128)S(1)} %get-tuple-element.11.p), custom_call_target="tpu_custom_call" | custom-call | tf_op jit(solution)/shard_map/pallas_call | solution.py:534
